TPU v7x, 32 devices: a whole 2x2x4 slice. The times are simulated.
32 devices in a mesh: mp: 2 (over core), tile: 16 (over z, y, x).
Axes of the slice: x: 2, y: 2, z: 4, core: 2. Of those that a mesh axis runs over, the one named last changes fastest.
Arguments:
- tracers: float32 [2, 4, 64, 256, 512], P('mp', None, None, 'tile'), may hold values from -6 to 6
- diffusivity: float32 [2, 63, 256, 512], P('mp', None, 'tile'), may hold values from 0.05 to 60
- conductance: float32 [2, 256, 512], P('mp', 'tile'), may hold values from 0.2 to 4
- face_velocity: float32 [2, 64, 256, 512], P('mp', None, 'tile'), may hold values from -0.3 to 0.3
- partner: int32 [2, 2, 256, 512], P('mp', None, 'tile'), may hold values from 0 to 255, as said below
- weight: int32 [2, 2, 256, 512], P('mp', None, 'tile'), may hold values from 0 to 15, as said below
- sea_mask: int32 [256, 512], P('tile'), may hold values from 0 to 1, as said below
Outputs:
- tracers_out: float32 [2, 4, 64, 256, 512], P('mp', None, None, 'tile')
- surface_inflow: float32 [2, 4, 256, 512], P('mp', None, 'tile')
Inputs may be any that keep to these rules, and one draw needn't show every extreme that they name: `partner`: entry [m, k, x, y] names a column of the other component in the same row y that intersects column (x, y) of component m, at most 9 cells from x along the periodic X direction; each intersection is listed on both sides with the same weight. `weight`: intersection area in units of 1 / 16 of a cell; 0 exactly where the ocean column of the intersection is land. `sea_mask`: 1 marks an ocean column, 0 land.
All inputs are finite; a program needn't handle non-finite values.
Results may differ from a plain program's by a relative error of at most 0.00002.
Values sent between devices are 32-bit elements; how exact they have to be, the bound alone decides.
No kernel may reach another device: no remote copies, remote signals or barrier semaphores. Data moves between devices by JAX's collectives and lax.ppermute only.
A program may use at most 192 MiB of HBM per device.

v0:
```python
import functools

import jax
import jax.numpy as jnp
from jax import lax
from jax.experimental import pallas as pl
from jax.experimental.pallas import tpu as pltpu
from jax.sharding import PartitionSpec as P

STEPS = 4
QUANT = 16
NU = 0.12
ROWS8 = 8
PARTS = (1, 1)
HALO = 2
F32 = jnp.float32
LITTLE = pl.CostEstimate(flops=1, bytes_accessed=1024, transcendentals=0)
VMEM = pl.BlockSpec(memory_space=pltpu.VMEM)
HBM = pl.BlockSpec(memory_space=pltpu.HBM)


def shape_of(*shape):
    return jax.ShapeDtypeStruct(shape, F32)


def params(mib):
    return pltpu.CompilerParams(vmem_limit_bytes=mib * 2**20)


def is_even():
    return lax.rem(lax.axis_index("tile"), 2) == 0


def either(even, call, first, second):
    @pl.when(even)
    def _():
        call(first, second)

    @pl.when(jnp.logical_not(even))
    def _():
        call(second, first)


def chunks_of(levels):
    sizes = [part * levels // sum(PARTS) for part in PARTS]
    return [(sum(sizes[:c]), size) for c, size in enumerate(sizes)]


def lane_parts(total, size=256):
    size = min(size, total)
    return [slice(start, start + size) for start in range(0, total, size)]


def down_kernel(reach, source, coupling, signed, order, parts, ratios, slope, terms, half_1, half_2, first_pair, second_pair, state, part_s, sems):
    tracers, levels, width, rows = source.shape
    blocks = levels // ROWS8

    def copies_of(b):
        part = pl.ds(b * ROWS8, ROWS8)
        return [pltpu.make_async_copy(source.at[t, part], parts.at[t, part], sems.at[b, t]) for t in range(tracers)]

    for b in range(blocks):
        for copy in copies_of(b):
            copy.start()
    state[...] = jnp.zeros_like(state)
    part_s[...] = jnp.zeros_like(part_s)

    def block(b, _):
        for copy in copies_of(b):
            copy.wait()
        for lanes in lane_parts(rows):
            before, ratio, inverse = [state[i, :, lanes] for i in range(3)]
            part = [part_s[t, :, lanes] for t in range(tracers)]
            for at in range(ROWS8):
                l = b * ROWS8 + at
                if at == ROWS8 - 1:
                    now = jnp.where(b == blocks - 1, 0.0, coupling[jnp.minimum(l, levels - 2), :, lanes])
                else:
                    now = coupling[l, :, lanes]
                inverse = 1.0 / (1.0 + before + now - before * ratio)
                part = [(parts[t, l, :, lanes] + before * part[t]) * inverse for t in range(tracers)]
                ratio = now * inverse
                before = now
                ratios[l, :, lanes] = ratio
                for t in range(tracers):
                    parts[t, l, :, lanes] = part[t]
            for i, value in enumerate((before, ratio, inverse)):
                state[i, :, lanes] = value
            for t in range(tracers):
                part_s[t, :, lanes] = part[t]
        return 0

    lax.fori_loop(0, blocks, block, 0)
    for t in range(tracers):
        terms[t] = part_s[t]
    slope[...] = state[2]
    terms[tracers] = 1.0 / jnp.abs(signed[...]) + state[2]
    half_1[...] = terms[:, : width // 2, :]
    half_2[...] = terms[:, width // 2 :, :]
    mask = jnp.where(signed[...] > 0.0, 1.0, 0.0)

    def pack(east, west):
        for c in range(tracers + 1):
            east[c * reach : (c + 1) * reach, :] = terms[c, width - reach :, :]
            west[c * reach : (c + 1) * reach, :] = terms[c, :reach, :]
        at = (tracers + 1) * reach
        east[at : at + HALO, :] = mask[width - HALO :]
        west[at : at + HALO, :] = mask[:HALO]

    either(is_even(), pack, first_pair, second_pair)


def down_to_surface(tracers, diffusivity, signed, order, reach):
    count, levels, width, rows = tracers.shape
    packed = (count + 1) * reach + HALO
    packed = -(-packed // 8) * 8
    return pl.pallas_call(
        functools.partial(down_kernel, reach),
        in_specs=[HBM, VMEM, VMEM, VMEM],
        out_specs=[VMEM] * 8,
        out_shape=[
            shape_of(count, levels, width, rows),
            shape_of(levels, width, rows),
            shape_of(width, rows),
            shape_of(count + 1, width, rows),
            shape_of(count + 1, width // 2, rows),
            shape_of(count + 1, width // 2, rows),
            shape_of(packed, rows),
            shape_of(packed, rows),
        ],
        scratch_shapes=[
            pltpu.VMEM((3, width, rows), F32),
            pltpu.VMEM((count, width, rows), F32),
            pltpu.SemaphoreType.DMA((levels // ROWS8, count)),
        ],
        compiler_params=params(41),
        cost_estimate=pl.CostEstimate(
            flops=20 * levels * width * rows, bytes_accessed=10 * levels * width * rows * 4, transcendentals=0
        ),
        name="down_to_surface",
    )(tracers, diffusivity, signed, order)


def up_kernel(rim, parts, ratios, arrived, fixed, scale, rims, rim_scale):
    tracers, levels, width, rows = parts.shape
    blocks = levels // ROWS8
    for lanes in lane_parts(rows):

        def block(i, state):
            b = blocks - 1 - i
            start = pl.multiple_of(b * ROWS8, ROWS8)
            scale_now, fixed_now = state[0], list(state[1:])
            for at in reversed(range(ROWS8)):
                l = start + at
                ratio = ratios[l, :, lanes]
                scale_now = ratio * scale_now
                fixed_now = [parts[t, l, :, lanes] + ratio * fixed_now[t] for t in range(tracers)]
                if at == ROWS8 - 1:
                    scale_now = jnp.where(i == 0, 1.0, scale_now)
                    fixed_now = [jnp.where(i == 0, 0.0, value) for value in fixed_now]
                scale[l, :, lanes] = scale_now
                for t in range(tracers):
                    fixed[t, l, :, lanes] = fixed_now[t]
                for c, x in enumerate(rim):
                    rim_scale[c, b, at : at + 1, lanes] = scale_now[x : x + 1]
                    for t in range(tracers):
                        rims[t, c, b, at : at + 1, lanes] = fixed_now[t][x : x + 1]
            return scale_now, *fixed_now

        zero = jnp.zeros((width, lanes.stop - lanes.start), F32)
        lax.fori_loop(0, blocks, block, (zero,) * (1 + tracers))


def speed_kernel(columns, speed, *out):
    out[-1][...] = jnp.zeros_like(out[-1])
    for l in range(speed.shape[0]):
        for ref, x in zip(out, columns):
            ref[l : l + 1, :] = speed[l, x : x + 1, :]


def speed_columns(speed, columns):
    levels, width, rows = speed.shape
    return pl.pallas_call(
        functools.partial(speed_kernel, columns),
        in_specs=[VMEM],
        out_specs=[VMEM] * (len(columns) + 1),
        out_shape=[shape_of(levels, rows)] * len(columns) + [shape_of(ROWS8, 128)],
        compiler_params=params(20),
        cost_estimate=LITTLE,
        name="speed_columns",
    )(speed)


def up_from_surface(parts, ratios, arrived, rim):
    count, levels, width, rows = parts.shape
    fixed, scale, rims, rim_scale = pl.pallas_call(
        functools.partial(up_kernel, rim),
        in_specs=[VMEM] * 3,
        out_specs=[VMEM] * 4,
        out_shape=[
            shape_of(count, levels, width, rows),
            shape_of(levels, width, rows),
            shape_of(count, len(rim), levels // ROWS8, ROWS8, rows),
            shape_of(len(rim), levels // ROWS8, ROWS8, rows),
        ],
        input_output_aliases={0: 0, 1: 1},
        compiler_params=params(20),
        cost_estimate=LITTLE,
        name="up_from_surface",
    )(parts, ratios, arrived)
    rims, rim_scale = rims.reshape(count, len(rim), levels, rows), rim_scale.reshape(len(rim), levels, rows)
    return fixed, scale, rims, rim_scale


def leaving(u, opening):
    return opening * (jnp.maximum(u, 0.0) + NU), opening * (jnp.minimum(u, 0.0) - NU)


def surface_kernel(
    reach, own, slope, peer_1, peer_2, first_pair, second_pair, partner, weight, signed, rims, rim_scale, speed_0, speed_1,
    inflow, surface, open_e, coef_n, *rest,
):
    chunks = chunks_of(rims.shape[2])
    send_1, send_2, wide, opened = rest[: len(chunks)], rest[len(chunks) : 2 * len(chunks)], rest[-2], rest[-1]
    channels, width, rows = own.shape
    tracers = channels - 1
    first = 2 * 8
    even = is_even()

    for c in range(channels):
        wide[c, first : first + width // 2, :] = peer_1[c]
        wide[c, first + width // 2 : first + width, :] = peer_2[c]
    opened[:width, :] = jnp.where(signed[...] > 0.0, 1.0, 0.0)
    opened[width:, :] = jnp.zeros((ROWS8, rows), F32)

    def unpack(east, west):
        for c in range(channels):
            part = slice(c * reach, (c + 1) * reach)
            wide[c, first - reach : first, :] = west[part, :]
            wide[c, first + width : first + width + reach, :] = east[part, :]
        at = slice(channels * reach, channels * reach + HALO)
        opened[width : width + HALO, :] = east[at, :]
        opened[width + ROWS8 - HALO :, :] = west[at, :]

    either(even, unpack, first_pair, second_pair)

    start = lax.axis_index("tile") * width
    total = lax.axis_size("tile") * width
    for lanes in lane_parts(rows, 128):
        position = start + lax.broadcasted_iota(jnp.int32, (width, 128), 0)
        own_rest = own[tracers, :, lanes]
        flow = [jnp.zeros((width, 128), F32) for _ in range(tracers)]
        for k in range(partner.shape[0]):
            apart = partner[k, :, lanes] - position
            apart = jnp.where(apart > reach, apart - total, apart)
            apart = jnp.where(apart < -reach, apart + total, apart)
            found = [jnp.zeros((width, 128), F32) for _ in range(channels)]
            for offset in range(-reach, reach + 1):
                hit = apart == offset
                window = slice(first + offset, first + offset + width)
                found = [jnp.where(hit, wide[c, window, lanes], f) for c, f in enumerate(found)]
            factor = weight[k, :, lanes].astype(F32) / (own_rest + found[-1])
            flow = [flow[t] + factor * (own[t, :, lanes] - found[t]) for t in range(tracers)]
        for t in range(tracers):
            into = flow[t] * (-1.0 / QUANT)
            inflow[t, :, lanes] = into
            surface[t, :, lanes] = own[t, :, lanes] + slope[:, lanes] * into

    wide_rows = width + ROWS8
    free = jnp.broadcast_to(lax.axis_index("mp"), (wide_rows, rows)) == 0
    here = jnp.where(free, 1.0, opened[...])
    column = lax.broadcasted_iota(jnp.int32, (wide_rows, rows), 1)
    open_e[...] = here * pltpu.roll(here, wide_rows - 1, 0)
    coef_n[...] = NU * (here * jnp.where(column == rows - 1, 0.0, pltpu.roll(here, rows - 1, 1)))

    for c, (begin, size) in enumerate(chunks):
        part = slice(begin, begin + size)
        faces_w = leaving(speed_0[part, :], open_e[:1, :])
        faces_e = leaving(speed_1[part, :], open_e[width - 2 : width - 1, :])
        for t in range(tracers):
            columns = []
            for i, x in enumerate((0, 1, width - 2, width - 1)):
                columns.append(rims[t, i, part, :] + rim_scale[i, part, :] * surface[t, x : x + 1, :])
            west = columns[0], faces_w[0] * columns[0] + faces_w[1] * columns[1]
            east = columns[3], faces_e[0] * columns[2] + faces_e[1] * columns[3]
            for i in range(2):
                send_1[c][t, i] = jnp.where(even, east[i], west[i])
                send_2[c][t, i] = jnp.where(even, west[i], east[i])


def exchange_surface(
    own, slope, peers, first_pair, second_pair, partner, weight, signed, rims, rim_scale, speeds, reach
):
    channels, width, rows = own.shape
    count, _, levels, _ = rims.shape
    plane = shape_of(width + ROWS8, rows)
    edges = [shape_of(count, 2, size, rows) for _, size in chunks_of(levels)]
    return pl.pallas_call(
        functools.partial(surface_kernel, reach),
        in_specs=[VMEM] * 13,
        out_specs=[VMEM] * (4 + 2 * len(edges)),
        out_shape=[shape_of(count, width, rows)] * 2 + [plane] * 2 + edges * 2,
        scratch_shapes=[pltpu.VMEM((channels, 16 + width + 16, rows), F32), pltpu.VMEM((width + ROWS8, rows), F32)],
        compiler_params=params(20),
        cost_estimate=LITTLE,
        name="exchange_surface",
    )(own, slope, *peers, first_pair, second_pair, partner, weight, signed, rims, rim_scale, *speeds)


def along_y(north, value):
    flux = north * (pltpu.roll(value, value.shape[-1] - 1, 1) - value)
    return flux - pltpu.roll(flux, 1, 1)


def inner_steps(q, a, b, north, width, put, keep):
    end = width - 1
    here, flux, once_before, flux_before = q(0), None, None, None
    for x in range(width):
        if x == 0:
            east = q(1)
            flux_e = a(0) * here + b(0) * east
            keep(0, here)
            keep(1, (here - flux_e) + along_y(north(0), here))
            once = None
        elif x == end:
            keep(4, here)
            keep(5, (here + flux) + along_y(north(end), here))
            keep(6, once_before)
            keep(7, (once_before + flux_before) + along_y(north(end - 1), once_before))
            break
        else:
            east = q(x + 1)
            flux_e = a(x) * here + b(x) * east
            once = (here - (flux_e - flux)) + along_y(north(x), here)
        if once_before is not None:
            flux_once = a(x - 1) * once_before + b(x - 1) * once
            second = along_y(north(x - 1), once_before)
            if flux_before is None:
                keep(2, once_before)
                keep(3, (once_before - flux_once) + second)
            else:
                put(x - 1, (once_before - (flux_once - flux_before)) + second)
            flux_before = flux_once
        here, flux, once_before = east, flux_e, once


def rim_steps(kept, west, east, a, b, north, width):
    end = width - 1
    value, behind = west
    flux = a(-1) * value + b(-1) * kept(0)
    outer = (value - (flux - behind)) + along_y(north(-1), value)
    edge = kept(1) + flux
    flux_out = a(-1) * outer + b(-1) * edge
    flux_in = a(0) * edge + b(0) * kept(2)
    new = {0: (edge - (flux_in - flux_out)) + along_y(north(0), edge), 1: kept(3) + flux_in}
    value, behind = east
    flux = a(end) * kept(4) + b(end) * value
    outer = (value - (behind - flux)) + along_y(north(width), value)
    edge = kept(5) - flux
    flux_out = a(end) * edge + b(end) * outer
    flux_in = a(end - 1) * kept(6) + b(end - 1) * edge
    new[end] = (edge - (flux_out - flux_in)) + along_y(north(end), edge)
    new[end - 1] = kept(7) - flux_in
    return new


def tiles_in(turn, value):
    levels, width, _ = value.shape
    for j in range(turn.shape[0]):
        turn[j] = value[:, :, 128 * j : 128 * (j + 1)].reshape(levels * width, 128)


def column(turn, x, width):
    parts = [turn[j, pl.ds(x, ROWS8, stride=width), :] for j in range(turn.shape[0])]
    return jnp.concatenate(parts, axis=1)


def put_column(stage, t, start, x, value):
    parts, tracers, levels, width, lanes = stage.shape
    rows = stage.reshape(parts, tracers, levels * width, lanes)
    for j in range(parts):
        at = pl.ds(start * width + x, ROWS8, stride=width)
        rows[j, t, at, :] = value[:, lanes * j : lanes * (j + 1)]


def ring(x, width):
    return x if x >= 0 else width + ROWS8 + x


def spread_north(coef_n, north_s, width):
    for x in range(1 - HALO, width + HALO - 1):
        row = ring(x, width)
        north_s[x + HALO] = jnp.broadcast_to(coef_n[row : row + 1, :], north_s.shape[1:])


def face(coefs, part, x, u, open_e, width):
    row = ring(x, width)
    coefs[0, x + 1, part, :], coefs[1, x + 1, part, :] = leaving(u, open_e[row : row + 1, :])


def faces(coefs, part):
    return [lambda x, i=i: coefs[i, x + 1, part, :] for i in range(2)]


def first_inner_kernel(
    begin, fixed, scale, surface, speed, open_e, coef_n,
    field, rims, coefs, coef_n_out, north_s, turn, turn_speed,
):
    tracers, levels, width, rows = fixed.shape
    size = field.shape[2]
    spread_north(coef_n, north_s, width)
    north = lambda x: north_s[x + HALO]

    def block(i, _):
        start = pl.multiple_of(i * ROWS8, ROWS8)
        part, whole = pl.ds(start, ROWS8), pl.ds(begin + start, ROWS8)
        tiles_in(turn_speed, speed[whole])
        for x in range(width):
            face(coefs, part, x, column(turn_speed, x, width), open_e, width)

        def tracer(t, _):
            tiles_in(turn, fixed[t, whole] + scale[whole] * surface[t][None])

            def put(x, value):
                field[t, x, part, :] = value

            def keep(i, value):
                rims[t, i, part, :] = value

            q = lambda x: column(turn, x, width)
            inner_steps(q, *faces(coefs, part), north, width, put, keep)
            return 0

        lax.fori_loop(0, tracers, tracer, 0)
        return 0

    lax.fori_loop(0, size // ROWS8, block, 0)


def halo_pair(even, halo_1, halo_2, t, part):
    pairs = [(halo_1[t, i, part, :], halo_2[t, i, part, :]) for i in range(2)]
    west = [jnp.where(even, second, first) for first, second in pairs]
    east = [jnp.where(even, first, second) for first, second in pairs]
    return west, east


def first_rim_kernel(
    begin, rims, speed_w, open_e, halo_1, halo_2, coef_n, field_in, coefs_in,
    field, coefs, send_1, send_2, coef_n_out, north_s,
):
    tracers, width, size, rows = field.shape
    even = is_even()
    spread_north(coef_n, north_s, width)
    north = lambda x: north_s[x + HALO]

    def block(i, _):
        start = pl.multiple_of(i * ROWS8, ROWS8)
        part, whole = pl.ds(start, ROWS8), pl.ds(begin + start, ROWS8)
        face(coefs, part, -1, speed_w[whole, :], open_e, width)
        a, b = faces(coefs, part)

        def tracer(t, _):
            halos = halo_pair(even, halo_1, halo_2, t, part)
            new = rim_steps(lambda i: rims[t, i, part, :], *halos, a, b, north, width)
            for x, value in new.items():
                field[t, x, part, :] = value
            end = width - 1
            west = new[0], a(0) * new[0] + b(0) * new[1]
            east = new[end], a(end - 1) * new[end - 1] + b(end - 1) * new[end]
            for i in range(2):
                send_1[t, i, part, :] = jnp.where(even, east[i], west[i])
                send_2[t, i, part, :] = jnp.where(even, west[i], east[i])
            return 0

        lax.fori_loop(0, tracers, tracer, 0)
        return 0

    lax.fori_loop(0, size // ROWS8, block, 0)


def last_inner_kernel(field, coefs, coef_n, stage, rims, coef_n_out, north_s):
    tracers, width, size, rows = field.shape
    spread_north(coef_n, north_s, width)
    north = lambda x: north_s[x + HALO]

    def block(i, _):
        start = pl.multiple_of(i * ROWS8, ROWS8)
        part = pl.ds(start, ROWS8)

        def tracer(t, _):
            q = lambda x: field[t, x, part, :]
            put = lambda x, value: put_column(stage, t, start, x, value)

            def keep(i, value):
                rims[t, i, part, :] = value

            inner_steps(q, *faces(coefs, part), north, width, put, keep)
            return 0

        lax.fori_loop(0, tracers, tracer, 0)
        return 0

    lax.fori_loop(0, size // ROWS8, block, 0)


def last_rim_kernel(begin, rims, coefs, halo_1, halo_2, coef_n, stage_in, *refs):
    out, stage, coef_n_out, north_s, sems = refs[-5:]
    _, tracers, size, width, _ = stage.shape
    even = is_even()
    spread_north(coef_n, north_s, width)
    north = lambda x: north_s[x + HALO]

    def copies_of(i):
        start = pl.multiple_of(i * ROWS8, ROWS8)
        part, to = pl.ds(start, ROWS8), pl.ds(begin + start, ROWS8)
        return [
            pltpu.make_async_copy(stage.at[j, :, part], out.at[:, to, :, pl.ds(128 * j, 128)], sems.at[i, j])
            for j in range(stage.shape[0])
        ]

    def block(i, _):
        start = pl.multiple_of(i * ROWS8, ROWS8)
        part = pl.ds(start, ROWS8)

        def tracer(t, _):
            halos = halo_pair(even, halo_1, halo_2, t, part)
            new = rim_steps(lambda i: rims[t, i, part, :], *halos, *faces(coefs, part), north, width)
            for x, value in new.items():
                put_column(stage, t, start, x, value)
            return 0

        lax.fori_loop(0, tracers, tracer, 0)
        for copy in copies_of(i):
            copy.start()
        return 0

    def finish(i, _):
        for copy in copies_of(i):
            copy.wait()
        return 0

    lax.fori_loop(0, size // ROWS8, block, 0)
    lax.fori_loop(0, size // ROWS8, finish, 0)


def transport_call(kernel, name, args, out_shape, aliases, scratch, cells, hbm=(), out_hbm=()):
    return pl.pallas_call(
        kernel,
        in_specs=[HBM if i in hbm else VMEM for i in range(len(args))],
        out_specs=[HBM if i in out_hbm else VMEM for i in range(len(out_shape))],
        out_shape=out_shape,
        scratch_shapes=scratch,
        input_output_aliases=aliases,
        compiler_params=params(16),
        cost_estimate=LITTLE,
        name=name,
    )(*args)


def north_scratch(width, rows):
    return pltpu.VMEM((width + 2 * HALO, ROWS8, rows), F32)


def first_inner(chunk, fixed, scale, surface, speed, open_e, coef_n):
    count, levels, width, rows = fixed.shape
    begin, size = chunk
    args = [fixed, scale, surface, speed, open_e, coef_n]
    out_shape = [
        shape_of(count, width, size, rows),
        shape_of(count, 8, size, rows),
        shape_of(2, width + 1, size, rows),
        shape_of(*coef_n.shape),
    ]
    turn = pltpu.VMEM((rows // 128, ROWS8 * width, 128), F32)
    return transport_call(
        functools.partial(first_inner_kernel, begin), "first_inner", args, out_shape, {len(args) - 1: 3},
        [north_scratch(width, rows), turn, turn], count * size * width * rows,
    )


def first_rim(chunk, field, rims, coefs, speed_w, open_e, halos, coef_n):
    count, width, size, rows = field.shape
    args = [rims, speed_w, open_e, *halos, coef_n, field, coefs]
    edge = shape_of(count, 2, size, rows)
    out_shape = [shape_of(*field.shape), shape_of(*coefs.shape), edge, edge, shape_of(*coef_n.shape)]
    field, coefs, send_1, send_2, coef_n = transport_call(
        functools.partial(first_rim_kernel, chunk[0]), "first_rim", args, out_shape, {5: 4, 6: 0, 7: 1},
        [north_scratch(width, rows)], count * size * 4 * rows,
    )
    return field, coefs, (send_1, send_2), coef_n


def last_inner(field, coefs, coef_n):
    count, width, size, rows = field.shape
    out_shape = [
        shape_of(rows // 128, count, size, width, 128),
        shape_of(count, 8, size, rows),
        shape_of(*coef_n.shape),
    ]
    return transport_call(
        last_inner_kernel, "last_inner", [field, coefs, coef_n], out_shape, {2: 2},
        [north_scratch(width, rows)], count * size * width * rows,
    )


def last_rim(chunk, levels, rims, coefs, halos, stage, coef_n, result):
    lane_tiles, count, size, width, lanes = stage.shape
    rows = lane_tiles * lanes
    args = [rims, coefs, *halos, coef_n, stage]
    aliases = {4: 2, 5: 1}
    if result is not None:
        aliases[6] = 0
        args.append(result)
    out_shape = [shape_of(count, levels, width, rows), shape_of(*stage.shape), shape_of(*coef_n.shape)]
    result, _, coef_n = transport_call(
        functools.partial(last_rim_kernel, chunk[0]), "last_rim", args, out_shape, aliases,
        [north_scratch(width, rows), pltpu.SemaphoreType.DMA((size // ROWS8, rows // 128))],
        count * size * 4 * rows, hbm=(6,), out_hbm=(0,),
    )
    return result, coef_n


def per_device(tracers, diffusivity, conductance, face_velocity, partner, weight, sea_mask):
    tiles = lax.axis_size("tile")
    tracers, diffusivity, conductance = tracers[0], diffusivity[0], conductance[0]
    speed, partner, weight = face_velocity[0], partner[0], weight[0]
    width = tracers.shape[2]
    reach = width // 2 + 1

    def move(value, target_of, swap=False):
        pairs = []
        for m in range(2):
            for t in range(tiles):
                target = (1 - m if swap else m) * tiles + target_of(t) % tiles
                pairs.append((m * tiles + t, target))
        return lax.ppermute(value, ("mp", "tile"), pairs)

    one = lambda t: t + 1 - 2 * (t % 2)
    two = lambda t: t - 1 + 2 * (t % 2)

    *speeds, to_east, order = speed_columns(speed, (0, width - 2, width - 1))
    speed_w = move(to_east, lambda t: t + 1)
    signed = jnp.where(sea_mask > 0, conductance, -conductance)
    parts, ratios, slope, own, *halves, terms_1, terms_2 = down_to_surface(tracers, diffusivity, signed, order, reach)
    terms_1 = move(terms_1, one, swap=True)
    terms_2 = move(terms_2, two, swap=True)
    peers = [move(half, lambda t: t, swap=True) for half in halves]
    rim = (0, 1, width - 2, width - 1)
    fixed, scale, rims, rim_scale = up_from_surface(parts, ratios, speed_w, rim)

    inflow, surface, open_e, coef_n, *sends = exchange_surface(
        own, slope, peers, terms_1, terms_2, partner, weight, signed, rims, rim_scale, speeds, reach
    )
    levels = fixed.shape[1]
    chunks = chunks_of(levels)
    every = range(len(chunks))
    exchange = lambda pair: (move(pair[0], one), move(pair[1], two))
    halos = [exchange((sends[c], sends[len(chunks) + c])) for c in every]
    fields, rims, coefs, stages = [[None] * len(chunks) for _ in range(4)]
    for c in every:
        fields[c], rims[c], coefs[c], coef_n = first_inner(chunks[c], fixed, scale, surface, speed, open_e, coef_n)
    for c in every:
        fields[c], coefs[c], pair, coef_n = first_rim(
            chunks[c], fields[c], rims[c], coefs[c], speed_w, open_e, halos[c], coef_n
        )
        halos[c] = exchange(pair)
    for c in every:
        stages[c], rims[c], coef_n = last_inner(fields[c], coefs[c], coef_n)
    result = None
    for c in every:
        result, coef_n = last_rim(chunks[c], levels, rims[c], coefs[c], halos[c], stages[c], coef_n, result)
    return result[None], inflow[None]


def solution(mesh):
    in_specs = (
        P("mp", None, None, "tile", None),
        P("mp", None, "tile", None),
        P("mp", "tile", None),
        P("mp", None, "tile", None),
        P("mp", None, "tile", None),
        P("mp", None, "tile", None),
        P("tile", None),
    )
    out_specs = (P("mp", None, None, "tile", None), P("mp", None, "tile", None))
    return jax.shard_map(
        per_device, mesh=mesh, in_specs=in_specs, out_specs=out_specs, check_vma=False
    )
```

profile of v0, /device:TPU:27, one launch (start us, length us, event | category | flops | bytes accessed | tf_op | source)
XLA Modules:
  0.0 117.3 jit_solution(10726727023560238465)
XLA Ops:
  0.6 0.0 copy-start
  0.6 1.6 %copy-done = f32[1,64,16,512]{3,2,1,0:T(8,128)S(1)} copy-done((f32[1,64,16,512]{3,2,1,0:T(8,128)S(1)}, f32[1,64,16,512]{3,2,1,0:T(8,128)}, u32[]{:S(2)}) %copy-start) | copy-done | bytes 2097176
  2.2 0.1 speed_columns.1
  2.3 1.3 %collective-permute-start = (f32[64,512]{1,0:T(8,128)S(1)}, f32[64,512]{1,0:T(8,128)S(1)}, u32[]{:S(2)}, u32[]{:S(2)}) collective-permute-start(f32[64,512]{1,0:T(8,128)S(1)} %get-tuple-element.56), channel_id=1, source_target_pairs={{0,1},{1,2},{2,3},{3,4},{4,5},{5,6},{6,7},{7,8},{8,9},{9,10},{10,1... | collective-permute-start | bytes 393224 | tf_op jit(solution)/shard_map/ppermute | solution.py:636
  3.6 0.8 negate_select_fusion.signed
  4.4 0.0 copy-start.2
  4.4 1.6 %copy-done.2 = f32[1,63,16,512]{3,2,1,0:T(8,128)S(1)} copy-done((f32[1,63,16,512]{3,2,1,0:T(8,128)S(1)}, f32[1,63,16,512]{3,2,1,0:T(8,128)}, u32[]{:S(2)}) %copy-start.2) | copy-done | bytes 2064408
  6.0 3.9 %down_to_surface.1 = (f32[4,64,16,512]{3,2,1,0:T(8,128)S(1)}, f32[64,16,512]{2,1,0:T(8,128)S(1)}, f32[16,512]{1,0:T(8,128)S(1)}, f32[5,16,512]{2,1,0:T(8,128)S(1...) custom-call(f32[4,64,16,512]{3,2,1,0:T(8,128)} %bitcast.20, ...), custom_call_target="tpu_custom_call" | custom-call | flops 10485760 | bytes 20971520 | tf_op jit(solution)/shard_map/down_to_surface/pallas_call | solution.py:117
  9.9 1.2 collective-permute-start.3
  11.0 1.0 collective-permute-start.4
  12.0 0.1 collective-permute-start.1
  12.1 0.5 collective-permute-start.2
  12.6 0.0 collective-permute-done.arrived.speed_w
  12.6 0.0 copy-start.3
  12.6 0.0 copy-start.4
  12.6 2.4 %up_from_surface.1 = (f32[4,64,16,512]{3,2,1,0:T(8,128)S(1)}, f32[64,16,512]{2,1,0:T(8,128)S(1)}, f32[4,4,8,8,512]{4,3,2,1,0:T(8,128)S(1)}, f32[4,8,8,512]{3,2,1,0:T(8,128)S(1)}) custom-call(f32[4,64,16,512]{3,2,1,0:T(8,128)S(1)} %get-tuple-element.54.parts, ...), custom_call_target="tpu_custom_call", output_to_operand_aliasing={{0}: (0, {}), {1}: (1, {})} | custom-call | flops 1 | bytes 1024 | tf_op jit(solution)/shard_map/up_from_surface/pallas_call | solution.py:196
  15.0 0.0 copy-start.1
  15.0 0.0 collective-permute-done.1.peer_1
  15.0 0.0 collective-permute-done.2.peer_2
  15.0 0.0 collective-permute-done.3.first_pair
  15.0 1.8 %collective-permute-done.4.second_pair = f32[48,512]{1,0:T(8,128)S(1)} collective-permute-done((f32[48,512]{1,0:T(8,128)S(1)}, f32[48,512]{1,0:T(8,128)S(1)}, u32[]{:S(2)}, u32[]{:S(2)}) %collective-permute-start.4) | collective-permute-done | bytes 98336 | tf_op jit(solution)/shard_map/ppermute | solution.py:636
  16.9 0.0 copy-done.3
  16.9 0.0 copy-done.4
  16.9 1.3 %exchange_surface.1 = (f32[4,16,512]{2,1,0:T(8,128)}, f32[4,16,512]{2,1,0:T(8,128)S(1)}, f32[24,512]{1,0:T(8,128)S(1)}, f32[24,512]{1,0:T(8,128)S(1)}, f32[4,2,3...) custom-call(f32[5,16,512]{2,1,0:T(8,128)S(1)} %get-tuple-element.59., ...), custom_call_target="tpu_custom_call" | custom-call | flops 1 | bytes 1024 | tf_op jit(solution)/shard_map/exchange_surface/pallas_call | solution.py:298
  18.2 1.3 %collective-permute-start.7 = (f32[4,2,32,512]{3,2,1,0:T(8,128)S(1)}, f32[4,2,32,512]{3,2,1,0:T(8,128)S(1)}, u32[]{:S(2)}, u32[]{:S(2)}) collective-permute-start(f32[4,2,32,512]{3,2,1,0:T(8,128)S(1)} %get-tuple-element.77), channel_id=1, source_target_pairs={{0,1},{1,0},{2,3},{3,2},{4,5},{5,4},{6,7},{7,6},{8,9},{9,8},{10,11... | collective-permute-start | bytes 1572872 | tf_op jit(solution)/shard_map/ppermute | solution.py:636
  19.5 2.9 %collective-permute-start.8 = (f32[4,2,32,512]{3,2,1,0:T(8,128)S(1)}, f32[4,2,32,512]{3,2,1,0:T(8,128)S(1)}, u32[]{:S(2)}, u32[]{:S(2)}) collective-permute-start(f32[4,2,32,512]{3,2,1,0:T(8,128)S(1)} %get-tuple-element.78), channel_id=1, source_target_pairs={{0,15},{1,2},{2,1},{3,4},{4,3},{5,6},{6,5},{7,8},{8,7},{9,10},{10,... | collective-permute-start | bytes 1572872 | tf_op jit(solution)/shard_map/ppermute | solution.py:636
  22.4 0.0 collective-permute-start.5
  22.4 0.8 collective-permute-start.6
  23.2 0.0 copy-done.1
  23.2 7.9 %first_inner.2 = (f32[4,16,32,512]{3,2,1,0:T(8,128)S(1)}, f32[4,8,32,512]{3,2,1,0:T(8,128)S(1)}, f32[2,17,32,512]{3,2,1,0:T(8,128)S(1)}, f32[24,512]{1,0:T(8,128)S(1)}) custom-call(f32[4,64,16,512]{3,2,1,0:T(8,128)S(1)} %get-tuple-element.57.fixed, f32[64,16,512]{2,1,0:T(8,128)S(1)} %get-tuple-element.58.scale, ...), custom_call_target="tpu_custom_call", output_to_operand_aliasing={{3}: (5, {})} | custom-call | flops 1 | bytes 1024 | tf_op jit(solution)/shard_map/first_inner/pallas_call | solution.py:547
  31.2 7.9 %first_inner.3 = (f32[4,16,32,512]{3,2,1,0:T(8,128)S(1)}, f32[4,8,32,512]{3,2,1,0:T(8,128)S(1)}, f32[2,17,32,512]{3,2,1,0:T(8,128)S(1)}, f32[24,512]{1,0:T(8,128)S(1)}) custom-call(f32[4,64,16,512]{3,2,1,0:T(8,128)S(1)} %get-tuple-element.57.fixed, f32[64,16,512]{2,1,0:T(8,128)S(1)} %get-tuple-element.58.scale, ...), custom_call_target="tpu_custom_call", output_to_operand_aliasing={{3}: (5, {})} | custom-call | flops 1 | bytes 1024 | tf_op jit(solution)/shard_map/first_inner/pallas_call | solution.py:547
  39.1 14.9 %collective-permute-done.7.halo_1 = f32[4,2,32,512]{3,2,1,0:T(8,128)S(1)} collective-permute-done((f32[4,2,32,512]{3,2,1,0:T(8,128)S(1)}, f32[4,2,32,512]{3,2,1,0:T(8,128)S(1)}, u32[]{:S(2)}, u32[]{:S(2)}) %collective-permute-start.7) | collective-permute-done | bytes 524320 | tf_op jit(solution)/shard_map/ppermute | solution.py:636
  54.0 0.0 collective-permute-done.8.halo_2
  54.0 2.7 %first_rim.2 = (f32[4,16,32,512]{3,2,1,0:T(8,128)S(1)}, f32[2,17,32,512]{3,2,1,0:T(8,128)S(1)}, f32[4,2,32,512]{3,2,1,0:T(8,128)S(1)}, f32[4,2,32,512]{3,2,1,0:T(8,128)S(1)}, f32[24,512]{1,0:T(8,128)S(1)}) custom-call(f32[4,8,32,512]{3,2,1,0:T(8,128)S(1)} %get-tuple-element.76.rims, ...), custom_call_target="tpu_custom_call", output_to_operand_aliasing={{4}: (5, {}), {0}: (6, {}), {1}: (7, {})} | custom-call | flops 1 | bytes 1024 | tf_op jit(solution)/shard_map/first_rim/pallas_call | solution.py:547
  56.7 0.1 collective-permute-start.11
  56.8 3.4 %collective-permute-start.12 = (f32[4,2,32,512]{3,2,1,0:T(8,128)S(1)}, f32[4,2,32,512]{3,2,1,0:T(8,128)S(1)}, u32[]{:S(2)}, u32[]{:S(2)}) collective-permute-start(f32[4,2,32,512]{3,2,1,0:T(8,128)S(1)} %get-tuple-element.96), channel_id=1, source_target_pairs={{0,15},{1,2},{2,1},{3,4},{4,3},{5,6},{6,5},{7,8},{8,7},{9,10},{10,... | collective-permute-start | bytes 1572872 | tf_op jit(solution)/shard_map/ppermute | solution.py:636
  60.2 5.1 %collective-permute-done.5.halo_1 = f32[4,2,32,512]{3,2,1,0:T(8,128)S(1)} collective-permute-done((f32[4,2,32,512]{3,2,1,0:T(8,128)S(1)}, f32[4,2,32,512]{3,2,1,0:T(8,128)S(1)}, u32[]{:S(2)}, u32[]{:S(2)}) %collective-permute-start.5) | collective-permute-done | bytes 524320 | tf_op jit(solution)/shard_map/ppermute | solution.py:636
  65.2 3.3 %collective-permute-done.6.halo_2 = f32[4,2,32,512]{3,2,1,0:T(8,128)S(1)} collective-permute-done((f32[4,2,32,512]{3,2,1,0:T(8,128)S(1)}, f32[4,2,32,512]{3,2,1,0:T(8,128)S(1)}, u32[]{:S(2)}, u32[]{:S(2)}) %collective-permute-start.6) | collective-permute-done | bytes 524320 | tf_op jit(solution)/shard_map/ppermute | solution.py:636
  68.6 2.7 %first_rim.3 = (f32[4,16,32,512]{3,2,1,0:T(8,128)S(1)}, f32[2,17,32,512]{3,2,1,0:T(8,128)S(1)}, f32[4,2,32,512]{3,2,1,0:T(8,128)S(1)}, f32[4,2,32,512]{3,2,1,0:T(8,128)S(1)}, f32[24,512]{1,0:T(8,128)S(1)}) custom-call(f32[4,8,32,512]{3,2,1,0:T(8,128)S(1)} %get-tuple-element.73.rims, ...), custom_call_target="tpu_custom_call", output_to_operand_aliasing={{4}: (5, {}), {0}: (6, {}), {1}: (7, {})} | custom-call | flops 1 | bytes 1024 | tf_op jit(solution)/shard_map/first_rim/pallas_call | solution.py:547
  71.3 0.1 collective-permute-start.9
  71.4 11.3 %collective-permute-start.10 = (f32[4,2,32,512]{3,2,1,0:T(8,128)S(1)}, f32[4,2,32,512]{3,2,1,0:T(8,128)S(1)}, u32[]{:S(2)}, u32[]{:S(2)}) collective-permute-start(f32[4,2,32,512]{3,2,1,0:T(8,128)S(1)} %get-tuple-element.93), channel_id=1, source_target_pairs={{0,15},{1,2},{2,1},{3,4},{4,3},{5,6},{6,5},{7,8},{8,7},{9,10},{10,... | collective-permute-start | bytes 1572872 | tf_op jit(solution)/shard_map/ppermute | solution.py:636
  82.7 7.7 %last_inner.2 = (f32[4,4,32,16,128]{4,3,2,1,0:T(8,128)S(1)}, f32[4,8,32,512]{3,2,1,0:T(8,128)S(1)}, f32[24,512]{1,0:T(8,128)S(1)}) custom-call(f32[4,16,32,512]{3,2,1,0:T(8,128)S(1)} %get-tuple-element.87.field, f32[2,17,32,512]{3,2,1,0:T(8,128)S(1)} %get-tuple-element.88.coefs, f32[24,512]{1,0:T(8,128)S(1)} %get-tuple-element.89.coef_n), custom_call_target="tpu_custom_call", output_to_operand_aliasing={{2}: (2, {})} | custom-call | flops 1 | bytes 1024 | tf_op jit(solution)/shard_map/last_inner/pallas_call | solution.py:547
  90.4 7.6 %last_inner.3 = (f32[4,4,32,16,128]{4,3,2,1,0:T(8,128)S(1)}, f32[4,8,32,512]{3,2,1,0:T(8,128)S(1)}, f32[24,512]{1,0:T(8,128)S(1)}) custom-call(f32[4,16,32,512]{3,2,1,0:T(8,128)S(1)} %get-tuple-element.85.field, f32[2,17,32,512]{3,2,1,0:T(8,128)S(1)} %get-tuple-element.86.coefs, f32[24,512]{1,0:T(8,128)S(1)} %get-tuple-element.90.coef_n), custom_call_target="tpu_custom_call", output_to_operand_aliasing={{2}: (2, {})} | custom-call | flops 1 | bytes 1024 | tf_op jit(solution)/shard_map/last_inner/pallas_call | solution.py:547
  98.0 0.0 collective-permute-done.11.halo_1
  98.0 0.0 collective-permute-done.12.halo_2
  98.0 3.8 %last_rim.2 = (f32[4,64,16,512]{3,2,1,0:T(8,128)}, f32[4,4,32,16,128]{4,3,2,1,0:T(8,128)S(1)}, f32[24,512]{1,0:T(8,128)S(1)}) custom-call(f32[4,8,32,512]{3,2,1,0:T(8,128)S(1)} %get-tuple-element.94.rims, f32[2,17,32,512]{3,2,1,0:T(8,128)S(1)} %get-tuple-element.88.coefs, ...), custom_call_target="tpu_custom_call", output_to_operand_aliasing={{2}: (4, {}), {1}: (5, {})} | custom-call | flops 1 | bytes 1024 | tf_op jit(solution)/shard_map/last_rim/pallas_call | solution.py:547
  101.8 8.3 %collective-permute-done.9.halo_1 = f32[4,2,32,512]{3,2,1,0:T(8,128)S(1)} collective-permute-done((f32[4,2,32,512]{3,2,1,0:T(8,128)S(1)}, f32[4,2,32,512]{3,2,1,0:T(8,128)S(1)}, u32[]{:S(2)}, u32[]{:S(2)}) %collective-permute-start.9) | collective-permute-done | bytes 524320 | tf_op jit(solution)/shard_map/ppermute | solution.py:636
  110.2 3.3 %collective-permute-done.10.halo_2 = f32[4,2,32,512]{3,2,1,0:T(8,128)S(1)} collective-permute-done((f32[4,2,32,512]{3,2,1,0:T(8,128)S(1)}, f32[4,2,32,512]{3,2,1,0:T(8,128)S(1)}, u32[]{:S(2)}, u32[]{:S(2)}) %collective-permute-start.10) | collective-permute-done | bytes 524320 | tf_op jit(solution)/shard_map/ppermute | solution.py:636
  113.5 3.8 %last_rim.3 = (f32[4,64,16,512]{3,2,1,0:T(8,128)}, f32[4,4,32,16,128]{4,3,2,1,0:T(8,128)S(1)}, f32[24,512]{1,0:T(8,128)S(1)}) custom-call(f32[4,8,32,512]{3,2,1,0:T(8,128)S(1)} %get-tuple-element.91.rims, f32[2,17,32,512]{3,2,1,0:T(8,128)S(1)} %get-tuple-element.86.coefs, ...), custom_call_target="tpu_custom_call", output_to_operand_aliasing={{2}: (4, {}), {1}: (5, {}), {0}: (6, {})} | custom-call | flops 1 | bytes 1024 | tf_op jit(solution)/shard_map/last_rim/pallas_call | solution.py:547
Async XLA Ops:
  0.6 1.6 %copy-start = (f32[1,64,16,512]{3,2,1,0:T(8,128)S(1)}, f32[1,64,16,512]{3,2,1,0:T(8,128)}, u32[]{:S(2)}) copy-start(f32[1,64,16,512]{3,2,1,0:T(8,128)} %param.10) | copy-start | bytes 6291460
  2.3 10.2 %collective-permute-start = (f32[64,512]{1,0:T(8,128)S(1)}, f32[64,512]{1,0:T(8,128)S(1)}, u32[]{:S(2)}, u32[]{:S(2)}) collective-permute-start(f32[64,512]{1,0:T(8,128)S(1)} %get-tuple-element.56), channel_id=1, source_target_pairs={{0,1},{1,2},{2,3},{3,4},{4,5},{5,6},{6,7},{7,8},{8,9},{9,10},{10,1... | collective-permute-start | bytes 393224 | tf_op jit(solution)/shard_map/ppermute | solution.py:636
  4.4 1.6 %copy-start.2 = (f32[1,63,16,512]{3,2,1,0:T(8,128)S(1)}, f32[1,63,16,512]{3,2,1,0:T(8,128)}, u32[]{:S(2)}) copy-start(f32[1,63,16,512]{3,2,1,0:T(8,128)} %param.8) | copy-start | bytes 6193156
  9.9 5.2 %collective-permute-start.3 = (f32[48,512]{1,0:T(8,128)S(1)}, f32[48,512]{1,0:T(8,128)S(1)}, u32[]{:S(2)}, u32[]{:S(2)}) collective-permute-start(f32[48,512]{1,0:T(8,128)S(1)} %get-tuple-element.63), channel_id=1, source_target_pairs={{0,17},{1,16},{2,19},{3,18},{4,21},{5,20},{6,23},{7,22},{8,25},{9,... | collective-permute-start | bytes 294920 | tf_op jit(solution)/shard_map/ppermute | solution.py:636
  11.0 5.9 %collective-permute-start.4 = (f32[48,512]{1,0:T(8,128)S(1)}, f32[48,512]{1,0:T(8,128)S(1)}, u32[]{:S(2)}, u32[]{:S(2)}) collective-permute-start(f32[48,512]{1,0:T(8,128)S(1)} %get-tuple-element.64), channel_id=1, source_target_pairs={{0,31},{1,18},{2,17},{3,20},{4,19},{5,22},{6,21},{7,24},{8,23},{9,... | collective-permute-start | bytes 294920 | tf_op jit(solution)/shard_map/ppermute | solution.py:636
  12.0 3.0 %collective-permute-start.1 = (f32[5,8,512]{2,1,0:T(8,128)S(1)}, f32[5,8,512]{2,1,0:T(8,128)S(1)}, u32[]{:S(2)}, u32[]{:S(2)}) collective-permute-start(f32[5,8,512]{2,1,0:T(8,128)S(1)} %get-tuple-element.61), channel_id=1, source_target_pairs={{0,16},{1,17},{2,18},{3,19},{4,20},{5,21},{6,22},{7,23},{8,24},{9,... | collective-permute-start | bytes 245768 | tf_op jit(solution)/shard_map/ppermute | solution.py:636
  12.1 2.9 %collective-permute-start.2 = (f32[5,8,512]{2,1,0:T(8,128)S(1)}, f32[5,8,512]{2,1,0:T(8,128)S(1)}, u32[]{:S(2)}, u32[]{:S(2)}) collective-permute-start(f32[5,8,512]{2,1,0:T(8,128)S(1)} %get-tuple-element.62), channel_id=1, source_target_pairs={{0,16},{1,17},{2,18},{3,19},{4,20},{5,21},{6,22},{7,23},{8,24},{9,... | collective-permute-start | bytes 245768 | tf_op jit(solution)/shard_map/ppermute | solution.py:636
  12.6 4.3 %copy-start.3 = (s32[1,2,16,512]{3,2,1,0:T(8,128)S(1)}, s32[1,2,16,512]{3,2,1,0:T(8,128)}, u32[]{:S(2)}) copy-start(s32[1,2,16,512]{3,2,1,0:T(8,128)} %param.11) | copy-start | bytes 196612
  12.6 4.3 %copy-start.4 = (s32[1,2,16,512]{3,2,1,0:T(8,128)S(1)}, s32[1,2,16,512]{3,2,1,0:T(8,128)}, u32[]{:S(2)}) copy-start(s32[1,2,16,512]{3,2,1,0:T(8,128)} %param.12) | copy-start | bytes 196612
  15.0 8.3 %copy-start.1 = (f32[1,64,16,512]{3,2,1,0:T(8,128)S(1)}, f32[1,64,16,512]{3,2,1,0:T(8,128)}, u32[]{:S(2)}) copy-start(f32[1,64,16,512]{3,2,1,0:T(8,128)} %param.10) | copy-start | bytes 6291460
  18.2 35.8 %collective-permute-start.7 = (f32[4,2,32,512]{3,2,1,0:T(8,128)S(1)}, f32[4,2,32,512]{3,2,1,0:T(8,128)S(1)}, u32[]{:S(2)}, u32[]{:S(2)}) collective-permute-start(f32[4,2,32,512]{3,2,1,0:T(8,128)S(1)} %get-tuple-element.77), channel_id=1, source_target_pairs={{0,1},{1,0},{2,3},{3,2},{4,5},{5,4},{6,7},{7,6},{8,9},{9,8},{10,11... | collective-permute-start | bytes 1572872 | tf_op jit(solution)/shard_map/ppermute | solution.py:636
  19.5 34.6 %collective-permute-start.8 = (f32[4,2,32,512]{3,2,1,0:T(8,128)S(1)}, f32[4,2,32,512]{3,2,1,0:T(8,128)S(1)}, u32[]{:S(2)}, u32[]{:S(2)}) collective-permute-start(f32[4,2,32,512]{3,2,1,0:T(8,128)S(1)} %get-tuple-element.78), channel_id=1, source_target_pairs={{0,15},{1,2},{2,1},{3,4},{4,3},{5,6},{6,5},{7,8},{8,7},{9,10},{10,... | collective-permute-start | bytes 1572872 | tf_op jit(solution)/shard_map/ppermute | solution.py:636
  22.4 42.8 %collective-permute-start.5 = (f32[4,2,32,512]{3,2,1,0:T(8,128)S(1)}, f32[4,2,32,512]{3,2,1,0:T(8,128)S(1)}, u32[]{:S(2)}, u32[]{:S(2)}) collective-permute-start(f32[4,2,32,512]{3,2,1,0:T(8,128)S(1)} %get-tuple-element.74), channel_id=1, source_target_pairs={{0,1},{1,0},{2,3},{3,2},{4,5},{5,4},{6,7},{7,6},{8,9},{9,8},{10,11... | collective-permute-start | bytes 1572872 | tf_op jit(solution)/shard_map/ppermute | solution.py:636
  22.4 46.2 %collective-permute-start.6 = (f32[4,2,32,512]{3,2,1,0:T(8,128)S(1)}, f32[4,2,32,512]{3,2,1,0:T(8,128)S(1)}, u32[]{:S(2)}, u32[]{:S(2)}) collective-permute-start(f32[4,2,32,512]{3,2,1,0:T(8,128)S(1)} %get-tuple-element.75), channel_id=1, source_target_pairs={{0,15},{1,2},{2,1},{3,4},{4,3},{5,6},{6,5},{7,8},{8,7},{9,10},{10,... | collective-permute-start | bytes 1572872 | tf_op jit(solution)/shard_map/ppermute | solution.py:636
  56.7 41.3 %collective-permute-start.11 = (f32[4,2,32,512]{3,2,1,0:T(8,128)S(1)}, f32[4,2,32,512]{3,2,1,0:T(8,128)S(1)}, u32[]{:S(2)}, u32[]{:S(2)}) collective-permute-start(f32[4,2,32,512]{3,2,1,0:T(8,128)S(1)} %get-tuple-element.95), channel_id=1, source_target_pairs={{0,1},{1,0},{2,3},{3,2},{4,5},{5,4},{6,7},{7,6},{8,9},{9,8},{10,11... | collective-permute-start | bytes 1572872 | tf_op jit(solution)/shard_map/ppermute | solution.py:636
  56.8 41.2 %collective-permute-start.12 = (f32[4,2,32,512]{3,2,1,0:T(8,128)S(1)}, f32[4,2,32,512]{3,2,1,0:T(8,128)S(1)}, u32[]{:S(2)}, u32[]{:S(2)}) collective-permute-start(f32[4,2,32,512]{3,2,1,0:T(8,128)S(1)} %get-tuple-element.96), channel_id=1, source_target_pairs={{0,15},{1,2},{2,1},{3,4},{4,3},{5,6},{6,5},{7,8},{8,7},{9,10},{10,... | collective-permute-start | bytes 1572872 | tf_op jit(solution)/shard_map/ppermute | solution.py:636
  71.3 38.9 %collective-permute-start.9 = (f32[4,2,32,512]{3,2,1,0:T(8,128)S(1)}, f32[4,2,32,512]{3,2,1,0:T(8,128)S(1)}, u32[]{:S(2)}, u32[]{:S(2)}) collective-permute-start(f32[4,2,32,512]{3,2,1,0:T(8,128)S(1)} %get-tuple-element.92), channel_id=1, source_target_pairs={{0,1},{1,0},{2,3},{3,2},{4,5},{5,4},{6,7},{7,6},{8,9},{9,8},{10,11... | collective-permute-start | bytes 1572872 | tf_op jit(solution)/shard_map/ppermute | solution.py:636
  71.4 42.2 %collective-permute-start.10 = (f32[4,2,32,512]{3,2,1,0:T(8,128)S(1)}, f32[4,2,32,512]{3,2,1,0:T(8,128)S(1)}, u32[]{:S(2)}, u32[]{:S(2)}) collective-permute-start(f32[4,2,32,512]{3,2,1,0:T(8,128)S(1)} %get-tuple-element.93), channel_id=1, source_target_pairs={{0,15},{1,2},{2,1},{3,4},{4,3},{5,6},{6,5},{7,8},{8,7},{9,10},{10,... | collective-permute-start | bytes 1572872 | tf_op jit(solution)/shard_map/ppermute | solution.py:636
where the time goes:
time: 118 us; the launch traced here: 117 us
  Pallas kernels  52 us (44%)
  waiting for transfers between devices  36.8 us (31%)
  starting transfers between devices  23.8 us (20%)
  local copies, waits for them, and re-layouts  3.18 us (3%)
    pallas_call x8, Pallas kernels, transport_call(): pl.pallas_call(kernel, in_specs=[HBM if i in hbm else VMEM for i in range...  44.2 us
    ppermute x13, waiting for transfers between devices, move(): return lax.ppermute(value, ('mp', 'tile'), pairs)  36.8 us
    ppermute x13, starting transfers between devices, move(): return lax.ppermute(value, ('mp', 'tile'), pairs)  23.8 us
    pallas_call x1, Pallas kernels, down_to_surface(): pl.pallas_call(functools.partial(down_kernel, reach), in_specs=[HBM, VMEM...  3.89 us
    unnamed x10, local copies, waits for them, and re-layouts  3.18 us
    pallas_call x1, Pallas kernels, up_from_surface(): pl.pallas_call(functools.partial(up_kernel, rim), in_specs=[VMEM] * 3, ou...  2.42 us
  transfers between devices with their start and end apart: 13, of which 6 were waited for; matrix products, arithmetic and copies ran while one was open for 1% of the time, Pallas kernels for 40%

commit v1 on v0

--- a/solution.py
+++ b/solution.py
@@ -367,7 +367,7 @@
 def tiles_in(turn, value):
     levels, width, _ = value.shape
     for j in range(turn.shape[0]):
-        turn[j] = value[:, :, 128 * j : 128 * (j + 1)].reshape(levels * width, 128)
+        turn[j, : levels * width, :] = value[:, :, 128 * j : 128 * (j + 1)].reshape(levels * width, 128)
 
 
 def column(turn, x, width):
@@ -505,7 +505,7 @@
 
 def last_rim_kernel(begin, rims, coefs, halo_1, halo_2, coef_n, stage_in, *refs):
     out, stage, coef_n_out, north_s, sems = refs[-5:]
-    _, tracers, size, width, _ = stage.shape
+    tracers, size, width = rims.shape[0], rims.shape[2], stage.shape[3]
     even = is_even()
     spread_north(coef_n, north_s, width)
     north = lambda x: north_s[x + HALO]
@@ -571,7 +571,7 @@
         shape_of(2, width + 1, size, rows),
         shape_of(*coef_n.shape),
     ]
-    turn = pltpu.VMEM((rows // 128, ROWS8 * width, 128), F32)
+    turn = pltpu.VMEM((rows // 128, (ROWS8 + 1) * width, 128), F32)
     return transport_call(
         functools.partial(first_inner_kernel, begin), "first_inner", args, out_shape, {len(args) - 1: 3},
         [north_scratch(width, rows), turn, turn], count * size * width * rows,
@@ -593,7 +593,7 @@
 def last_inner(field, coefs, coef_n):
     count, width, size, rows = field.shape
     out_shape = [
-        shape_of(rows // 128, count, size, width, 128),
+        shape_of(rows // 128, count, size + 1, width, 128),
         shape_of(count, 8, size, rows),
         shape_of(*coef_n.shape),
     ]
@@ -604,8 +604,8 @@
 
 
 def last_rim(chunk, levels, rims, coefs, halos, stage, coef_n, result):
-    lane_tiles, count, size, width, lanes = stage.shape
-    rows = lane_tiles * lanes
+    count, _, size, rows = rims.shape
+    width = stage.shape[3]
     args = [rims, coefs, *halos, coef_n, stage]
     aliases = {4: 2, 5: 1}
     if result is not None:

time: 118 us -> 118 us (level)
  no operation moved by 1% of the time
where the time goes in v1:
time: 118 us; the launch traced here: 117 us
  Pallas kernels  52.1 us (44%)
  waiting for transfers between devices  36.6 us (31%)
  starting transfers between devices  23.8 us (20%)
  local copies, waits for them, and re-layouts  3.18 us (3%)
    pallas_call x8, Pallas kernels, transport_call(): pl.pallas_call(kernel, in_specs=[HBM if i in hbm else VMEM for i in range...  44.4 us
    ppermute x13, waiting for transfers between devices, move(): return lax.ppermute(value, ('mp', 'tile'), pairs)  36.6 us
    ppermute x13, starting transfers between devices, move(): return lax.ppermute(value, ('mp', 'tile'), pairs)  23.8 us
    pallas_call x1, Pallas kernels, down_to_surface(): pl.pallas_call(functools.partial(down_kernel, reach), in_specs=[HBM, VMEM...  3.89 us
    unnamed x10, local copies, waits for them, and re-layouts  3.18 us
    pallas_call x1, Pallas kernels, up_from_surface(): pl.pallas_call(functools.partial(up_kernel, rim), in_specs=[VMEM] * 3, ou...  2.42 us
  transfers between devices with their start and end apart: 13, of which 6 were waited for; matrix products, arithmetic and copies ran while one was open for 1% of the time, Pallas kernels for 40%

profile of v1, /device:TPU:27, one launch (start us, length us, event | category | flops | bytes accessed | tf_op | source)
XLA Modules:
  0.0 117.3 jit_solution(3266799508620433534)
XLA Ops:
  0.6 0.0 copy-start
  0.6 1.6 %copy-done = f32[1,64,16,512]{3,2,1,0:T(8,128)S(1)} copy-done((f32[1,64,16,512]{3,2,1,0:T(8,128)S(1)}, f32[1,64,16,512]{3,2,1,0:T(8,128)}, u32[]{:S(2)}) %copy-start) | copy-done | bytes 2097176
  2.2 0.1 speed_columns.1
  2.3 1.3 %collective-permute-start = (f32[64,512]{1,0:T(8,128)S(1)}, f32[64,512]{1,0:T(8,128)S(1)}, u32[]{:S(2)}, u32[]{:S(2)}) collective-permute-start(f32[64,512]{1,0:T(8,128)S(1)} %get-tuple-element.56), channel_id=1, source_target_pairs={{0,1},{1,2},{2,3},{3,4},{4,5},{5,6},{6,7},{7,8},{8,9},{9,10},{10,1... | collective-permute-start | bytes 393224 | tf_op jit(solution)/shard_map/ppermute | solution.py:636
  3.6 0.8 negate_select_fusion.signed
  4.4 0.0 copy-start.2
  4.4 1.6 %copy-done.2 = f32[1,63,16,512]{3,2,1,0:T(8,128)S(1)} copy-done((f32[1,63,16,512]{3,2,1,0:T(8,128)S(1)}, f32[1,63,16,512]{3,2,1,0:T(8,128)}, u32[]{:S(2)}) %copy-start.2) | copy-done | bytes 2064408
  6.0 3.9 %down_to_surface.1 = (f32[4,64,16,512]{3,2,1,0:T(8,128)S(1)}, f32[64,16,512]{2,1,0:T(8,128)S(1)}, f32[16,512]{1,0:T(8,128)S(1)}, f32[5,16,512]{2,1,0:T(8,128)S(1...) custom-call(f32[4,64,16,512]{3,2,1,0:T(8,128)} %bitcast.20, ...), custom_call_target="tpu_custom_call" | custom-call | flops 10485760 | bytes 20971520 | tf_op jit(solution)/shard_map/down_to_surface/pallas_call | solution.py:117
  9.9 1.2 collective-permute-start.3
  11.0 1.0 collective-permute-start.4
  12.0 0.1 collective-permute-start.1
  12.1 0.5 collective-permute-start.2
  12.6 0.0 collective-permute-done.arrived.speed_w
  12.6 0.0 copy-start.3
  12.6 0.0 copy-start.4
  12.6 2.4 %up_from_surface.1 = (f32[4,64,16,512]{3,2,1,0:T(8,128)S(1)}, f32[64,16,512]{2,1,0:T(8,128)S(1)}, f32[4,4,8,8,512]{4,3,2,1,0:T(8,128)S(1)}, f32[4,8,8,512]{3,2,1,0:T(8,128)S(1)}) custom-call(f32[4,64,16,512]{3,2,1,0:T(8,128)S(1)} %get-tuple-element.54.parts, ...), custom_call_target="tpu_custom_call", output_to_operand_aliasing={{0}: (0, {}), {1}: (1, {})} | custom-call | flops 1 | bytes 1024 | tf_op jit(solution)/shard_map/up_from_surface/pallas_call | solution.py:196
  15.0 0.0 copy-start.1
  15.0 0.0 collective-permute-done.1.peer_1
  15.0 0.0 collective-permute-done.2.peer_2
  15.0 0.0 collective-permute-done.3.first_pair
  15.0 1.8 %collective-permute-done.4.second_pair = f32[48,512]{1,0:T(8,128)S(1)} collective-permute-done((f32[48,512]{1,0:T(8,128)S(1)}, f32[48,512]{1,0:T(8,128)S(1)}, u32[]{:S(2)}, u32[]{:S(2)}) %collective-permute-start.4) | collective-permute-done | bytes 98336 | tf_op jit(solution)/shard_map/ppermute | solution.py:636
  16.9 0.0 copy-done.3
  16.9 0.0 copy-done.4
  16.9 1.3 %exchange_surface.1 = (f32[4,16,512]{2,1,0:T(8,128)}, f32[4,16,512]{2,1,0:T(8,128)S(1)}, f32[24,512]{1,0:T(8,128)S(1)}, f32[24,512]{1,0:T(8,128)S(1)}, f32[4,2,3...) custom-call(f32[5,16,512]{2,1,0:T(8,128)S(1)} %get-tuple-element.59., ...), custom_call_target="tpu_custom_call" | custom-call | flops 1 | bytes 1024 | tf_op jit(solution)/shard_map/exchange_surface/pallas_call | solution.py:298
  18.2 1.3 %collective-permute-start.7 = (f32[4,2,32,512]{3,2,1,0:T(8,128)S(1)}, f32[4,2,32,512]{3,2,1,0:T(8,128)S(1)}, u32[]{:S(2)}, u32[]{:S(2)}) collective-permute-start(f32[4,2,32,512]{3,2,1,0:T(8,128)S(1)} %get-tuple-element.77), channel_id=1, source_target_pairs={{0,1},{1,0},{2,3},{3,2},{4,5},{5,4},{6,7},{7,6},{8,9},{9,8},{10,11... | collective-permute-start | bytes 1572872 | tf_op jit(solution)/shard_map/ppermute | solution.py:636
  19.5 2.9 %collective-permute-start.8 = (f32[4,2,32,512]{3,2,1,0:T(8,128)S(1)}, f32[4,2,32,512]{3,2,1,0:T(8,128)S(1)}, u32[]{:S(2)}, u32[]{:S(2)}) collective-permute-start(f32[4,2,32,512]{3,2,1,0:T(8,128)S(1)} %get-tuple-element.78), channel_id=1, source_target_pairs={{0,15},{1,2},{2,1},{3,4},{4,3},{5,6},{6,5},{7,8},{8,7},{9,10},{10,... | collective-permute-start | bytes 1572872 | tf_op jit(solution)/shard_map/ppermute | solution.py:636
  22.4 0.0 collective-permute-start.5
  22.4 0.8 collective-permute-start.6
  23.2 0.0 copy-done.1
  23.2 7.9 %first_inner.2 = (f32[4,16,32,512]{3,2,1,0:T(8,128)S(1)}, f32[4,8,32,512]{3,2,1,0:T(8,128)S(1)}, f32[2,17,32,512]{3,2,1,0:T(8,128)S(1)}, f32[24,512]{1,0:T(8,128)S(1)}) custom-call(f32[4,64,16,512]{3,2,1,0:T(8,128)S(1)} %get-tuple-element.57.fixed, f32[64,16,512]{2,1,0:T(8,128)S(1)} %get-tuple-element.58.scale, ...), custom_call_target="tpu_custom_call", output_to_operand_aliasing={{3}: (5, {})} | custom-call | flops 1 | bytes 1024 | tf_op jit(solution)/shard_map/first_inner/pallas_call | solution.py:547
  31.2 8.0 %first_inner.3 = (f32[4,16,32,512]{3,2,1,0:T(8,128)S(1)}, f32[4,8,32,512]{3,2,1,0:T(8,128)S(1)}, f32[2,17,32,512]{3,2,1,0:T(8,128)S(1)}, f32[24,512]{1,0:T(8,128)S(1)}) custom-call(f32[4,64,16,512]{3,2,1,0:T(8,128)S(1)} %get-tuple-element.57.fixed, f32[64,16,512]{2,1,0:T(8,128)S(1)} %get-tuple-element.58.scale, ...), custom_call_target="tpu_custom_call", output_to_operand_aliasing={{3}: (5, {})} | custom-call | flops 1 | bytes 1024 | tf_op jit(solution)/shard_map/first_inner/pallas_call | solution.py:547
  39.1 14.9 %collective-permute-done.7.halo_1 = f32[4,2,32,512]{3,2,1,0:T(8,128)S(1)} collective-permute-done((f32[4,2,32,512]{3,2,1,0:T(8,128)S(1)}, f32[4,2,32,512]{3,2,1,0:T(8,128)S(1)}, u32[]{:S(2)}, u32[]{:S(2)}) %collective-permute-start.7) | collective-permute-done | bytes 524320 | tf_op jit(solution)/shard_map/ppermute | solution.py:636
  54.0 0.0 collective-permute-done.8.halo_2
  54.0 2.7 %first_rim.2 = (f32[4,16,32,512]{3,2,1,0:T(8,128)S(1)}, f32[2,17,32,512]{3,2,1,0:T(8,128)S(1)}, f32[4,2,32,512]{3,2,1,0:T(8,128)S(1)}, f32[4,2,32,512]{3,2,1,0:T(8,128)S(1)}, f32[24,512]{1,0:T(8,128)S(1)}) custom-call(f32[4,8,32,512]{3,2,1,0:T(8,128)S(1)} %get-tuple-element.76.rims, ...), custom_call_target="tpu_custom_call", output_to_operand_aliasing={{4}: (5, {}), {0}: (6, {}), {1}: (7, {})} | custom-call | flops 1 | bytes 1024 | tf_op jit(solution)/shard_map/first_rim/pallas_call | solution.py:547
  56.7 0.1 collective-permute-start.11
  56.8 3.4 %collective-permute-start.12 = (f32[4,2,32,512]{3,2,1,0:T(8,128)S(1)}, f32[4,2,32,512]{3,2,1,0:T(8,128)S(1)}, u32[]{:S(2)}, u32[]{:S(2)}) collective-permute-start(f32[4,2,32,512]{3,2,1,0:T(8,128)S(1)} %get-tuple-element.96), channel_id=1, source_target_pairs={{0,15},{1,2},{2,1},{3,4},{4,3},{5,6},{6,5},{7,8},{8,7},{9,10},{10,... | collective-permute-start | bytes 1572872 | tf_op jit(solution)/shard_map/ppermute | solution.py:636
  60.2 5.1 %collective-permute-done.5.halo_1 = f32[4,2,32,512]{3,2,1,0:T(8,128)S(1)} collective-permute-done((f32[4,2,32,512]{3,2,1,0:T(8,128)S(1)}, f32[4,2,32,512]{3,2,1,0:T(8,128)S(1)}, u32[]{:S(2)}, u32[]{:S(2)}) %collective-permute-start.5) | collective-permute-done | bytes 524320 | tf_op jit(solution)/shard_map/ppermute | solution.py:636
  65.2 3.3 %collective-permute-done.6.halo_2 = f32[4,2,32,512]{3,2,1,0:T(8,128)S(1)} collective-permute-done((f32[4,2,32,512]{3,2,1,0:T(8,128)S(1)}, f32[4,2,32,512]{3,2,1,0:T(8,128)S(1)}, u32[]{:S(2)}, u32[]{:S(2)}) %collective-permute-start.6) | collective-permute-done | bytes 524320 | tf_op jit(solution)/shard_map/ppermute | solution.py:636
  68.6 2.7 %first_rim.3 = (f32[4,16,32,512]{3,2,1,0:T(8,128)S(1)}, f32[2,17,32,512]{3,2,1,0:T(8,128)S(1)}, f32[4,2,32,512]{3,2,1,0:T(8,128)S(1)}, f32[4,2,32,512]{3,2,1,0:T(8,128)S(1)}, f32[24,512]{1,0:T(8,128)S(1)}) custom-call(f32[4,8,32,512]{3,2,1,0:T(8,128)S(1)} %get-tuple-element.73.rims, ...), custom_call_target="tpu_custom_call", output_to_operand_aliasing={{4}: (5, {}), {0}: (6, {}), {1}: (7, {})} | custom-call | flops 1 | bytes 1024 | tf_op jit(solution)/shard_map/first_rim/pallas_call | solution.py:547
  71.3 0.1 collective-permute-start.9
  71.4 11.3 %collective-permute-start.10 = (f32[4,2,32,512]{3,2,1,0:T(8,128)S(1)}, f32[4,2,32,512]{3,2,1,0:T(8,128)S(1)}, u32[]{:S(2)}, u32[]{:S(2)}) collective-permute-start(f32[4,2,32,512]{3,2,1,0:T(8,128)S(1)} %get-tuple-element.93), channel_id=1, source_target_pairs={{0,15},{1,2},{2,1},{3,4},{4,3},{5,6},{6,5},{7,8},{8,7},{9,10},{10,... | collective-permute-start | bytes 1572872 | tf_op jit(solution)/shard_map/ppermute | solution.py:636
  82.7 7.7 %last_inner.2 = (f32[4,4,33,16,128]{4,3,2,1,0:T(8,128)S(1)}, f32[4,8,32,512]{3,2,1,0:T(8,128)S(1)}, f32[24,512]{1,0:T(8,128)S(1)}) custom-call(f32[4,16,32,512]{3,2,1,0:T(8,128)S(1)} %get-tuple-element.87.field, f32[2,17,32,512]{3,2,1,0:T(8,128)S(1)} %get-tuple-element.88.coefs, f32[24,512]{1,0:T(8,128)S(1)} %get-tuple-element.89.coef_n), custom_call_target="tpu_custom_call", output_to_operand_aliasing={{2}: (2, {})} | custom-call | flops 1 | bytes 1024 | tf_op jit(solution)/shard_map/last_inner/pallas_call | solution.py:547
  90.4 7.7 %last_inner.3 = (f32[4,4,33,16,128]{4,3,2,1,0:T(8,128)S(1)}, f32[4,8,32,512]{3,2,1,0:T(8,128)S(1)}, f32[24,512]{1,0:T(8,128)S(1)}) custom-call(f32[4,16,32,512]{3,2,1,0:T(8,128)S(1)} %get-tuple-element.85.field, f32[2,17,32,512]{3,2,1,0:T(8,128)S(1)} %get-tuple-element.86.coefs, f32[24,512]{1,0:T(8,128)S(1)} %get-tuple-element.90.coef_n), custom_call_target="tpu_custom_call", output_to_operand_aliasing={{2}: (2, {})} | custom-call | flops 1 | bytes 1024 | tf_op jit(solution)/shard_map/last_inner/pallas_call | solution.py:547
  98.1 0.0 collective-permute-done.11.halo_1
  98.1 0.0 collective-permute-done.12.halo_2
  98.1 3.8 %last_rim.2 = (f32[4,64,16,512]{3,2,1,0:T(8,128)}, f32[4,4,33,16,128]{4,3,2,1,0:T(8,128)S(1)}, f32[24,512]{1,0:T(8,128)S(1)}) custom-call(f32[4,8,32,512]{3,2,1,0:T(8,128)S(1)} %get-tuple-element.94.rims, f32[2,17,32,512]{3,2,1,0:T(8,128)S(1)} %get-tuple-element.88.coefs, ...), custom_call_target="tpu_custom_call", output_to_operand_aliasing={{2}: (4, {}), {1}: (5, {})} | custom-call | flops 1 | bytes 1024 | tf_op jit(solution)/shard_map/last_rim/pallas_call | solution.py:547
  102.0 8.2 %collective-permute-done.9.halo_1 = f32[4,2,32,512]{3,2,1,0:T(8,128)S(1)} collective-permute-done((f32[4,2,32,512]{3,2,1,0:T(8,128)S(1)}, f32[4,2,32,512]{3,2,1,0:T(8,128)S(1)}, u32[]{:S(2)}, u32[]{:S(2)}) %collective-permute-start.9) | collective-permute-done | bytes 524320 | tf_op jit(solution)/shard_map/ppermute | solution.py:636
  110.2 3.3 %collective-permute-done.10.halo_2 = f32[4,2,32,512]{3,2,1,0:T(8,128)S(1)} collective-permute-done((f32[4,2,32,512]{3,2,1,0:T(8,128)S(1)}, f32[4,2,32,512]{3,2,1,0:T(8,128)S(1)}, u32[]{:S(2)}, u32[]{:S(2)}) %collective-permute-start.10) | collective-permute-done | bytes 524320 | tf_op jit(solution)/shard_map/ppermute | solution.py:636
  113.5 3.8 %last_rim.3 = (f32[4,64,16,512]{3,2,1,0:T(8,128)}, f32[4,4,33,16,128]{4,3,2,1,0:T(8,128)S(1)}, f32[24,512]{1,0:T(8,128)S(1)}) custom-call(f32[4,8,32,512]{3,2,1,0:T(8,128)S(1)} %get-tuple-element.91.rims, f32[2,17,32,512]{3,2,1,0:T(8,128)S(1)} %get-tuple-element.86.coefs, ...), custom_call_target="tpu_custom_call", output_to_operand_aliasing={{2}: (4, {}), {1}: (5, {}), {0}: (6, {})} | custom-call | flops 1 | bytes 1024 | tf_op jit(solution)/shard_map/last_rim/pallas_call | solution.py:547
Async XLA Ops:
  0.6 1.6 %copy-start = (f32[1,64,16,512]{3,2,1,0:T(8,128)S(1)}, f32[1,64,16,512]{3,2,1,0:T(8,128)}, u32[]{:S(2)}) copy-start(f32[1,64,16,512]{3,2,1,0:T(8,128)} %param.10) | copy-start | bytes 6291460
  2.3 10.2 %collective-permute-start = (f32[64,512]{1,0:T(8,128)S(1)}, f32[64,512]{1,0:T(8,128)S(1)}, u32[]{:S(2)}, u32[]{:S(2)}) collective-permute-start(f32[64,512]{1,0:T(8,128)S(1)} %get-tuple-element.56), channel_id=1, source_target_pairs={{0,1},{1,2},{2,3},{3,4},{4,5},{5,6},{6,7},{7,8},{8,9},{9,10},{10,1... | collective-permute-start | bytes 393224 | tf_op jit(solution)/shard_map/ppermute | solution.py:636
  4.4 1.6 %copy-start.2 = (f32[1,63,16,512]{3,2,1,0:T(8,128)S(1)}, f32[1,63,16,512]{3,2,1,0:T(8,128)}, u32[]{:S(2)}) copy-start(f32[1,63,16,512]{3,2,1,0:T(8,128)} %param.8) | copy-start | bytes 6193156
  9.9 5.2 %collective-permute-start.3 = (f32[48,512]{1,0:T(8,128)S(1)}, f32[48,512]{1,0:T(8,128)S(1)}, u32[]{:S(2)}, u32[]{:S(2)}) collective-permute-start(f32[48,512]{1,0:T(8,128)S(1)} %get-tuple-element.63), channel_id=1, source_target_pairs={{0,17},{1,16},{2,19},{3,18},{4,21},{5,20},{6,23},{7,22},{8,25},{9,... | collective-permute-start | bytes 294920 | tf_op jit(solution)/shard_map/ppermute | solution.py:636
  11.0 5.9 %collective-permute-start.4 = (f32[48,512]{1,0:T(8,128)S(1)}, f32[48,512]{1,0:T(8,128)S(1)}, u32[]{:S(2)}, u32[]{:S(2)}) collective-permute-start(f32[48,512]{1,0:T(8,128)S(1)} %get-tuple-element.64), channel_id=1, source_target_pairs={{0,31},{1,18},{2,17},{3,20},{4,19},{5,22},{6,21},{7,24},{8,23},{9,... | collective-permute-start | bytes 294920 | tf_op jit(solution)/shard_map/ppermute | solution.py:636
  12.0 3.0 %collective-permute-start.1 = (f32[5,8,512]{2,1,0:T(8,128)S(1)}, f32[5,8,512]{2,1,0:T(8,128)S(1)}, u32[]{:S(2)}, u32[]{:S(2)}) collective-permute-start(f32[5,8,512]{2,1,0:T(8,128)S(1)} %get-tuple-element.61), channel_id=1, source_target_pairs={{0,16},{1,17},{2,18},{3,19},{4,20},{5,21},{6,22},{7,23},{8,24},{9,... | collective-permute-start | bytes 245768 | tf_op jit(solution)/shard_map/ppermute | solution.py:636
  12.1 2.9 %collective-permute-start.2 = (f32[5,8,512]{2,1,0:T(8,128)S(1)}, f32[5,8,512]{2,1,0:T(8,128)S(1)}, u32[]{:S(2)}, u32[]{:S(2)}) collective-permute-start(f32[5,8,512]{2,1,0:T(8,128)S(1)} %get-tuple-element.62), channel_id=1, source_target_pairs={{0,16},{1,17},{2,18},{3,19},{4,20},{5,21},{6,22},{7,23},{8,24},{9,... | collective-permute-start | bytes 245768 | tf_op jit(solution)/shard_map/ppermute | solution.py:636
  12.6 4.3 %copy-start.3 = (s32[1,2,16,512]{3,2,1,0:T(8,128)S(1)}, s32[1,2,16,512]{3,2,1,0:T(8,128)}, u32[]{:S(2)}) copy-start(s32[1,2,16,512]{3,2,1,0:T(8,128)} %param.11) | copy-start | bytes 196612
  12.6 4.3 %copy-start.4 = (s32[1,2,16,512]{3,2,1,0:T(8,128)S(1)}, s32[1,2,16,512]{3,2,1,0:T(8,128)}, u32[]{:S(2)}) copy-start(s32[1,2,16,512]{3,2,1,0:T(8,128)} %param.12) | copy-start | bytes 196612
  15.0 8.3 %copy-start.1 = (f32[1,64,16,512]{3,2,1,0:T(8,128)S(1)}, f32[1,64,16,512]{3,2,1,0:T(8,128)}, u32[]{:S(2)}) copy-start(f32[1,64,16,512]{3,2,1,0:T(8,128)} %param.10) | copy-start | bytes 6291460
  18.2 35.8 %collective-permute-start.7 = (f32[4,2,32,512]{3,2,1,0:T(8,128)S(1)}, f32[4,2,32,512]{3,2,1,0:T(8,128)S(1)}, u32[]{:S(2)}, u32[]{:S(2)}) collective-permute-start(f32[4,2,32,512]{3,2,1,0:T(8,128)S(1)} %get-tuple-element.77), channel_id=1, source_target_pairs={{0,1},{1,0},{2,3},{3,2},{4,5},{5,4},{6,7},{7,6},{8,9},{9,8},{10,11... | collective-permute-start | bytes 1572872 | tf_op jit(solution)/shard_map/ppermute | solution.py:636
  19.5 34.6 %collective-permute-start.8 = (f32[4,2,32,512]{3,2,1,0:T(8,128)S(1)}, f32[4,2,32,512]{3,2,1,0:T(8,128)S(1)}, u32[]{:S(2)}, u32[]{:S(2)}) collective-permute-start(f32[4,2,32,512]{3,2,1,0:T(8,128)S(1)} %get-tuple-element.78), channel_id=1, source_target_pairs={{0,15},{1,2},{2,1},{3,4},{4,3},{5,6},{6,5},{7,8},{8,7},{9,10},{10,... | collective-permute-start | bytes 1572872 | tf_op jit(solution)/shard_map/ppermute | solution.py:636
  22.4 42.8 %collective-permute-start.5 = (f32[4,2,32,512]{3,2,1,0:T(8,128)S(1)}, f32[4,2,32,512]{3,2,1,0:T(8,128)S(1)}, u32[]{:S(2)}, u32[]{:S(2)}) collective-permute-start(f32[4,2,32,512]{3,2,1,0:T(8,128)S(1)} %get-tuple-element.74), channel_id=1, source_target_pairs={{0,1},{1,0},{2,3},{3,2},{4,5},{5,4},{6,7},{7,6},{8,9},{9,8},{10,11... | collective-permute-start | bytes 1572872 | tf_op jit(solution)/shard_map/ppermute | solution.py:636
  22.4 46.2 %collective-permute-start.6 = (f32[4,2,32,512]{3,2,1,0:T(8,128)S(1)}, f32[4,2,32,512]{3,2,1,0:T(8,128)S(1)}, u32[]{:S(2)}, u32[]{:S(2)}) collective-permute-start(f32[4,2,32,512]{3,2,1,0:T(8,128)S(1)} %get-tuple-element.75), channel_id=1, source_target_pairs={{0,15},{1,2},{2,1},{3,4},{4,3},{5,6},{6,5},{7,8},{8,7},{9,10},{10,... | collective-permute-start | bytes 1572872 | tf_op jit(solution)/shard_map/ppermute | solution.py:636
  56.7 41.4 %collective-permute-start.11 = (f32[4,2,32,512]{3,2,1,0:T(8,128)S(1)}, f32[4,2,32,512]{3,2,1,0:T(8,128)S(1)}, u32[]{:S(2)}, u32[]{:S(2)}) collective-permute-start(f32[4,2,32,512]{3,2,1,0:T(8,128)S(1)} %get-tuple-element.95), channel_id=1, source_target_pairs={{0,1},{1,0},{2,3},{3,2},{4,5},{5,4},{6,7},{7,6},{8,9},{9,8},{10,11... | collective-permute-start | bytes 1572872 | tf_op jit(solution)/shard_map/ppermute | solution.py:636
  56.8 41.3 %collective-permute-start.12 = (f32[4,2,32,512]{3,2,1,0:T(8,128)S(1)}, f32[4,2,32,512]{3,2,1,0:T(8,128)S(1)}, u32[]{:S(2)}, u32[]{:S(2)}) collective-permute-start(f32[4,2,32,512]{3,2,1,0:T(8,128)S(1)} %get-tuple-element.96), channel_id=1, source_target_pairs={{0,15},{1,2},{2,1},{3,4},{4,3},{5,6},{6,5},{7,8},{8,7},{9,10},{10,... | collective-permute-start | bytes 1572872 | tf_op jit(solution)/shard_map/ppermute | solution.py:636
  71.3 38.9 %collective-permute-start.9 = (f32[4,2,32,512]{3,2,1,0:T(8,128)S(1)}, f32[4,2,32,512]{3,2,1,0:T(8,128)S(1)}, u32[]{:S(2)}, u32[]{:S(2)}) collective-permute-start(f32[4,2,32,512]{3,2,1,0:T(8,128)S(1)} %get-tuple-element.92), channel_id=1, source_target_pairs={{0,1},{1,0},{2,3},{3,2},{4,5},{5,4},{6,7},{7,6},{8,9},{9,8},{10,11... | collective-permute-start | bytes 1572872 | tf_op jit(solution)/shard_map/ppermute | solution.py:636
  71.4 42.2 %collective-permute-start.10 = (f32[4,2,32,512]{3,2,1,0:T(8,128)S(1)}, f32[4,2,32,512]{3,2,1,0:T(8,128)S(1)}, u32[]{:S(2)}, u32[]{:S(2)}) collective-permute-start(f32[4,2,32,512]{3,2,1,0:T(8,128)S(1)} %get-tuple-element.93), channel_id=1, source_target_pairs={{0,15},{1,2},{2,1},{3,4},{4,3},{5,6},{6,5},{7,8},{8,7},{9,10},{10,... | collective-permute-start | bytes 1572872 | tf_op jit(solution)/shard_map/ppermute | solution.py:636

commit v2 on v1

--- a/solution.py
+++ b/solution.py
@@ -387,8 +387,8 @@
     return x if x >= 0 else width + ROWS8 + x
 
 
-def spread_north(coef_n, north_s, width):
-    for x in range(1 - HALO, width + HALO - 1):
+def spread_north(coef_n, north_s, width, columns=None):
+    for x in columns or range(width):
         row = ring(x, width)
         north_s[x + HALO] = jnp.broadcast_to(coef_n[row : row + 1, :], north_s.shape[1:])
 
@@ -450,7 +450,7 @@
 ):
     tracers, width, size, rows = field.shape
     even = is_even()
-    spread_north(coef_n, north_s, width)
+    spread_north(coef_n, north_s, width, (-1, 0, width - 1, width))
     north = lambda x: north_s[x + HALO]
 
     def block(i, _):
@@ -507,14 +507,14 @@
     out, stage, coef_n_out, north_s, sems = refs[-5:]
     tracers, size, width = rims.shape[0], rims.shape[2], stage.shape[3]
     even = is_even()
-    spread_north(coef_n, north_s, width)
+    spread_north(coef_n, north_s, width, (-1, 0, width - 1, width))
     north = lambda x: north_s[x + HALO]
 
-    def copies_of(i):
+    def copies_of(i, t):
         start = pl.multiple_of(i * ROWS8, ROWS8)
         part, to = pl.ds(start, ROWS8), pl.ds(begin + start, ROWS8)
         return [
-            pltpu.make_async_copy(stage.at[j, :, part], out.at[:, to, :, pl.ds(128 * j, 128)], sems.at[i, j])
+            pltpu.make_async_copy(stage.at[j, t, part], out.at[t, to, :, pl.ds(128 * j, 128)], sems.at[i, t, j])
             for j in range(stage.shape[0])
         ]
 
@@ -527,16 +527,17 @@
             new = rim_steps(lambda i: rims[t, i, part, :], *halos, *faces(coefs, part), north, width)
             for x, value in new.items():
                 put_column(stage, t, start, x, value)
+            for copy in copies_of(i, t):
+                copy.start()
             return 0
 
         lax.fori_loop(0, tracers, tracer, 0)
-        for copy in copies_of(i):
-            copy.start()
         return 0
 
     def finish(i, _):
-        for copy in copies_of(i):
-            copy.wait()
+        for t in range(tracers):
+            for copy in copies_of(i, t):
+                copy.wait()
         return 0
 
     lax.fori_loop(0, size // ROWS8, block, 0)
@@ -614,7 +615,7 @@
     out_shape = [shape_of(count, levels, width, rows), shape_of(*stage.shape), shape_of(*coef_n.shape)]
     result, _, coef_n = transport_call(
         functools.partial(last_rim_kernel, chunk[0]), "last_rim", args, out_shape, aliases,
-        [north_scratch(width, rows), pltpu.SemaphoreType.DMA((size // ROWS8, rows // 128))],
+        [north_scratch(width, rows), pltpu.SemaphoreType.DMA((size // ROWS8, count, rows // 128))],
         count * size * 4 * rows, hbm=(6,), out_hbm=(0,),
     )
     return result, coef_n

time: 118 us -> 118 us (level)
  no operation moved by 1% of the time
where the time goes in v2:
time: 118 us
  Pallas kernels  52.5 us (44%)
  waiting for transfers between devices  36.5 us (31%)
  starting transfers between devices  23.8 us (20%)
  local copies, waits for them, and re-layouts  3.18 us (3%)
    pallas_call x8, Pallas kernels, transport_call(): pl.pallas_call(kernel, in_specs=[HBM if i in hbm else VMEM for i in range...  44.7 us
    ppermute x13, waiting for transfers between devices, move(): return lax.ppermute(value, ('mp', 'tile'), pairs)  36.5 us
    ppermute x13, starting transfers between devices, move(): return lax.ppermute(value, ('mp', 'tile'), pairs)  23.8 us
    pallas_call x1, Pallas kernels, down_to_surface(): pl.pallas_call(functools.partial(down_kernel, reach), in_specs=[HBM, VMEM...  3.89 us
    unnamed x10, local copies, waits for them, and re-layouts  3.18 us
    pallas_call x1, Pallas kernels, up_from_surface(): pl.pallas_call(functools.partial(up_kernel, rim), in_specs=[VMEM] * 3, ou...  2.42 us
  transfers between devices with their start and end apart: 13, of which 6 were waited for; matrix products, arithmetic and copies ran while one was open for 1% of the time, Pallas kernels for 40%

profile of v2, /device:TPU:27, one launch (start us, length us, event | category | flops | bytes accessed | tf_op | source)
XLA Modules:
  0.0 117.5 jit_solution(13347125105384166511)
XLA Ops:
  0.6 0.0 copy-start
  0.6 1.6 %copy-done = f32[1,64,16,512]{3,2,1,0:T(8,128)S(1)} copy-done((f32[1,64,16,512]{3,2,1,0:T(8,128)S(1)}, f32[1,64,16,512]{3,2,1,0:T(8,128)}, u32[]{:S(2)}) %copy-start) | copy-done | bytes 2097176
  2.2 0.1 speed_columns.1
  2.3 1.3 %collective-permute-start = (f32[64,512]{1,0:T(8,128)S(1)}, f32[64,512]{1,0:T(8,128)S(1)}, u32[]{:S(2)}, u32[]{:S(2)}) collective-permute-start(f32[64,512]{1,0:T(8,128)S(1)} %get-tuple-element.56), channel_id=1, source_target_pairs={{0,1},{1,2},{2,3},{3,4},{4,5},{5,6},{6,7},{7,8},{8,9},{9,10},{10,1... | collective-permute-start | bytes 393224 | tf_op jit(solution)/shard_map/ppermute | solution.py:637
  3.6 0.8 negate_select_fusion.signed
  4.4 0.0 copy-start.2
  4.4 1.6 %copy-done.2 = f32[1,63,16,512]{3,2,1,0:T(8,128)S(1)} copy-done((f32[1,63,16,512]{3,2,1,0:T(8,128)S(1)}, f32[1,63,16,512]{3,2,1,0:T(8,128)}, u32[]{:S(2)}) %copy-start.2) | copy-done | bytes 2064408
  6.0 3.9 %down_to_surface.1 = (f32[4,64,16,512]{3,2,1,0:T(8,128)S(1)}, f32[64,16,512]{2,1,0:T(8,128)S(1)}, f32[16,512]{1,0:T(8,128)S(1)}, f32[5,16,512]{2,1,0:T(8,128)S(1...) custom-call(f32[4,64,16,512]{3,2,1,0:T(8,128)} %bitcast.20, ...), custom_call_target="tpu_custom_call" | custom-call | flops 10485760 | bytes 20971520 | tf_op jit(solution)/shard_map/down_to_surface/pallas_call | solution.py:117
  9.9 1.2 collective-permute-start.3
  11.0 1.0 collective-permute-start.4
  12.0 0.1 collective-permute-start.1
  12.1 0.5 collective-permute-start.2
  12.6 0.0 collective-permute-done.arrived.speed_w
  12.6 0.0 copy-start.3
  12.6 0.0 copy-start.4
  12.6 2.4 %up_from_surface.1 = (f32[4,64,16,512]{3,2,1,0:T(8,128)S(1)}, f32[64,16,512]{2,1,0:T(8,128)S(1)}, f32[4,4,8,8,512]{4,3,2,1,0:T(8,128)S(1)}, f32[4,8,8,512]{3,2,1,0:T(8,128)S(1)}) custom-call(f32[4,64,16,512]{3,2,1,0:T(8,128)S(1)} %get-tuple-element.54.parts, ...), custom_call_target="tpu_custom_call", output_to_operand_aliasing={{0}: (0, {}), {1}: (1, {})} | custom-call | flops 1 | bytes 1024 | tf_op jit(solution)/shard_map/up_from_surface/pallas_call | solution.py:196
  15.0 0.0 copy-start.1
  15.0 0.0 collective-permute-done.1.peer_1
  15.0 0.0 collective-permute-done.2.peer_2
  15.0 0.0 collective-permute-done.3.first_pair
  15.0 1.8 %collective-permute-done.4.second_pair = f32[48,512]{1,0:T(8,128)S(1)} collective-permute-done((f32[48,512]{1,0:T(8,128)S(1)}, f32[48,512]{1,0:T(8,128)S(1)}, u32[]{:S(2)}, u32[]{:S(2)}) %collective-permute-start.4) | collective-permute-done | bytes 98336 | tf_op jit(solution)/shard_map/ppermute | solution.py:637
  16.9 0.0 copy-done.3
  16.9 0.0 copy-done.4
  16.9 1.3 %exchange_surface.1 = (f32[4,16,512]{2,1,0:T(8,128)}, f32[4,16,512]{2,1,0:T(8,128)S(1)}, f32[24,512]{1,0:T(8,128)S(1)}, f32[24,512]{1,0:T(8,128)S(1)}, f32[4,2,3...) custom-call(f32[5,16,512]{2,1,0:T(8,128)S(1)} %get-tuple-element.59., ...), custom_call_target="tpu_custom_call" | custom-call | flops 1 | bytes 1024 | tf_op jit(solution)/shard_map/exchange_surface/pallas_call | solution.py:298
  18.2 1.3 %collective-permute-start.7 = (f32[4,2,32,512]{3,2,1,0:T(8,128)S(1)}, f32[4,2,32,512]{3,2,1,0:T(8,128)S(1)}, u32[]{:S(2)}, u32[]{:S(2)}) collective-permute-start(f32[4,2,32,512]{3,2,1,0:T(8,128)S(1)} %get-tuple-element.77), channel_id=1, source_target_pairs={{0,1},{1,0},{2,3},{3,2},{4,5},{5,4},{6,7},{7,6},{8,9},{9,8},{10,11... | collective-permute-start | bytes 1572872 | tf_op jit(solution)/shard_map/ppermute | solution.py:637
  19.5 2.9 %collective-permute-start.8 = (f32[4,2,32,512]{3,2,1,0:T(8,128)S(1)}, f32[4,2,32,512]{3,2,1,0:T(8,128)S(1)}, u32[]{:S(2)}, u32[]{:S(2)}) collective-permute-start(f32[4,2,32,512]{3,2,1,0:T(8,128)S(1)} %get-tuple-element.78), channel_id=1, source_target_pairs={{0,15},{1,2},{2,1},{3,4},{4,3},{5,6},{6,5},{7,8},{8,7},{9,10},{10,... | collective-permute-start | bytes 1572872 | tf_op jit(solution)/shard_map/ppermute | solution.py:637
  22.4 0.0 collective-permute-start.5
  22.4 0.8 collective-permute-start.6
  23.2 0.0 copy-done.1
  23.2 7.9 %first_inner.2 = (f32[4,16,32,512]{3,2,1,0:T(8,128)S(1)}, f32[4,8,32,512]{3,2,1,0:T(8,128)S(1)}, f32[2,17,32,512]{3,2,1,0:T(8,128)S(1)}, f32[24,512]{1,0:T(8,128)S(1)}) custom-call(f32[4,64,16,512]{3,2,1,0:T(8,128)S(1)} %get-tuple-element.57.fixed, f32[64,16,512]{2,1,0:T(8,128)S(1)} %get-tuple-element.58.scale, ...), custom_call_target="tpu_custom_call", output_to_operand_aliasing={{3}: (5, {})} | custom-call | flops 1 | bytes 1024 | tf_op jit(solution)/shard_map/first_inner/pallas_call | solution.py:548
  31.2 8.0 %first_inner.3 = (f32[4,16,32,512]{3,2,1,0:T(8,128)S(1)}, f32[4,8,32,512]{3,2,1,0:T(8,128)S(1)}, f32[2,17,32,512]{3,2,1,0:T(8,128)S(1)}, f32[24,512]{1,0:T(8,128)S(1)}) custom-call(f32[4,64,16,512]{3,2,1,0:T(8,128)S(1)} %get-tuple-element.57.fixed, f32[64,16,512]{2,1,0:T(8,128)S(1)} %get-tuple-element.58.scale, ...), custom_call_target="tpu_custom_call", output_to_operand_aliasing={{3}: (5, {})} | custom-call | flops 1 | bytes 1024 | tf_op jit(solution)/shard_map/first_inner/pallas_call | solution.py:548
  39.1 14.9 %collective-permute-done.7.halo_1 = f32[4,2,32,512]{3,2,1,0:T(8,128)S(1)} collective-permute-done((f32[4,2,32,512]{3,2,1,0:T(8,128)S(1)}, f32[4,2,32,512]{3,2,1,0:T(8,128)S(1)}, u32[]{:S(2)}, u32[]{:S(2)}) %collective-permute-start.7) | collective-permute-done | bytes 524320 | tf_op jit(solution)/shard_map/ppermute | solution.py:637
  54.0 0.0 collective-permute-done.8.halo_2
  54.0 2.7 %first_rim.2 = (f32[4,16,32,512]{3,2,1,0:T(8,128)S(1)}, f32[2,17,32,512]{3,2,1,0:T(8,128)S(1)}, f32[4,2,32,512]{3,2,1,0:T(8,128)S(1)}, f32[4,2,32,512]{3,2,1,0:T(8,128)S(1)}, f32[24,512]{1,0:T(8,128)S(1)}) custom-call(f32[4,8,32,512]{3,2,1,0:T(8,128)S(1)} %get-tuple-element.76.rims, ...), custom_call_target="tpu_custom_call", output_to_operand_aliasing={{4}: (5, {}), {0}: (6, {}), {1}: (7, {})} | custom-call | flops 1 | bytes 1024 | tf_op jit(solution)/shard_map/first_rim/pallas_call | solution.py:548
  56.7 0.1 collective-permute-start.11
  56.8 3.4 %collective-permute-start.12 = (f32[4,2,32,512]{3,2,1,0:T(8,128)S(1)}, f32[4,2,32,512]{3,2,1,0:T(8,128)S(1)}, u32[]{:S(2)}, u32[]{:S(2)}) collective-permute-start(f32[4,2,32,512]{3,2,1,0:T(8,128)S(1)} %get-tuple-element.96), channel_id=1, source_target_pairs={{0,15},{1,2},{2,1},{3,4},{4,3},{5,6},{6,5},{7,8},{8,7},{9,10},{10,... | collective-permute-start | bytes 1572872 | tf_op jit(solution)/shard_map/ppermute | solution.py:637
  60.2 5.1 %collective-permute-done.5.halo_1 = f32[4,2,32,512]{3,2,1,0:T(8,128)S(1)} collective-permute-done((f32[4,2,32,512]{3,2,1,0:T(8,128)S(1)}, f32[4,2,32,512]{3,2,1,0:T(8,128)S(1)}, u32[]{:S(2)}, u32[]{:S(2)}) %collective-permute-start.5) | collective-permute-done | bytes 524320 | tf_op jit(solution)/shard_map/ppermute | solution.py:637
  65.2 3.3 %collective-permute-done.6.halo_2 = f32[4,2,32,512]{3,2,1,0:T(8,128)S(1)} collective-permute-done((f32[4,2,32,512]{3,2,1,0:T(8,128)S(1)}, f32[4,2,32,512]{3,2,1,0:T(8,128)S(1)}, u32[]{:S(2)}, u32[]{:S(2)}) %collective-permute-start.6) | collective-permute-done | bytes 524320 | tf_op jit(solution)/shard_map/ppermute | solution.py:637
  68.6 2.7 %first_rim.3 = (f32[4,16,32,512]{3,2,1,0:T(8,128)S(1)}, f32[2,17,32,512]{3,2,1,0:T(8,128)S(1)}, f32[4,2,32,512]{3,2,1,0:T(8,128)S(1)}, f32[4,2,32,512]{3,2,1,0:T(8,128)S(1)}, f32[24,512]{1,0:T(8,128)S(1)}) custom-call(f32[4,8,32,512]{3,2,1,0:T(8,128)S(1)} %get-tuple-element.73.rims, ...), custom_call_target="tpu_custom_call", output_to_operand_aliasing={{4}: (5, {}), {0}: (6, {}), {1}: (7, {})} | custom-call | flops 1 | bytes 1024 | tf_op jit(solution)/shard_map/first_rim/pallas_call | solution.py:548
  71.3 0.1 collective-permute-start.9
  71.4 11.3 %collective-permute-start.10 = (f32[4,2,32,512]{3,2,1,0:T(8,128)S(1)}, f32[4,2,32,512]{3,2,1,0:T(8,128)S(1)}, u32[]{:S(2)}, u32[]{:S(2)}) collective-permute-start(f32[4,2,32,512]{3,2,1,0:T(8,128)S(1)} %get-tuple-element.93), channel_id=1, source_target_pairs={{0,15},{1,2},{2,1},{3,4},{4,3},{5,6},{6,5},{7,8},{8,7},{9,10},{10,... | collective-permute-start | bytes 1572872 | tf_op jit(solution)/shard_map/ppermute | solution.py:637
  82.7 7.7 %last_inner.2 = (f32[4,4,33,16,128]{4,3,2,1,0:T(8,128)S(1)}, f32[4,8,32,512]{3,2,1,0:T(8,128)S(1)}, f32[24,512]{1,0:T(8,128)S(1)}) custom-call(f32[4,16,32,512]{3,2,1,0:T(8,128)S(1)} %get-tuple-element.87.field, f32[2,17,32,512]{3,2,1,0:T(8,128)S(1)} %get-tuple-element.88.coefs, f32[24,512]{1,0:T(8,128)S(1)} %get-tuple-element.89.coef_n), custom_call_target="tpu_custom_call", output_to_operand_aliasing={{2}: (2, {})} | custom-call | flops 1 | bytes 1024 | tf_op jit(solution)/shard_map/last_inner/pallas_call | solution.py:548
  90.4 7.7 %last_inner.3 = (f32[4,4,33,16,128]{4,3,2,1,0:T(8,128)S(1)}, f32[4,8,32,512]{3,2,1,0:T(8,128)S(1)}, f32[24,512]{1,0:T(8,128)S(1)}) custom-call(f32[4,16,32,512]{3,2,1,0:T(8,128)S(1)} %get-tuple-element.85.field, f32[2,17,32,512]{3,2,1,0:T(8,128)S(1)} %get-tuple-element.86.coefs, f32[24,512]{1,0:T(8,128)S(1)} %get-tuple-element.90.coef_n), custom_call_target="tpu_custom_call", output_to_operand_aliasing={{2}: (2, {})} | custom-call | flops 1 | bytes 1024 | tf_op jit(solution)/shard_map/last_inner/pallas_call | solution.py:548
  98.1 0.0 collective-permute-done.11.halo_1
  98.1 0.0 collective-permute-done.12.halo_2
  98.1 4.0 %last_rim.2 = (f32[4,64,16,512]{3,2,1,0:T(8,128)}, f32[4,4,33,16,128]{4,3,2,1,0:T(8,128)S(1)}, f32[24,512]{1,0:T(8,128)S(1)}) custom-call(f32[4,8,32,512]{3,2,1,0:T(8,128)S(1)} %get-tuple-element.94.rims, f32[2,17,32,512]{3,2,1,0:T(8,128)S(1)} %get-tuple-element.88.coefs, ...), custom_call_target="tpu_custom_call", output_to_operand_aliasing={{2}: (4, {}), {1}: (5, {})} | custom-call | flops 1 | bytes 1024 | tf_op jit(solution)/shard_map/last_rim/pallas_call | solution.py:548
  102.1 8.0 %collective-permute-done.9.halo_1 = f32[4,2,32,512]{3,2,1,0:T(8,128)S(1)} collective-permute-done((f32[4,2,32,512]{3,2,1,0:T(8,128)S(1)}, f32[4,2,32,512]{3,2,1,0:T(8,128)S(1)}, u32[]{:S(2)}, u32[]{:S(2)}) %collective-permute-start.9) | collective-permute-done | bytes 524320 | tf_op jit(solution)/shard_map/ppermute | solution.py:637
  110.2 3.3 %collective-permute-done.10.halo_2 = f32[4,2,32,512]{3,2,1,0:T(8,128)S(1)} collective-permute-done((f32[4,2,32,512]{3,2,1,0:T(8,128)S(1)}, f32[4,2,32,512]{3,2,1,0:T(8,128)S(1)}, u32[]{:S(2)}, u32[]{:S(2)}) %collective-permute-start.10) | collective-permute-done | bytes 524320 | tf_op jit(solution)/shard_map/ppermute | solution.py:637
  113.5 4.0 %last_rim.3 = (f32[4,64,16,512]{3,2,1,0:T(8,128)}, f32[4,4,33,16,128]{4,3,2,1,0:T(8,128)S(1)}, f32[24,512]{1,0:T(8,128)S(1)}) custom-call(f32[4,8,32,512]{3,2,1,0:T(8,128)S(1)} %get-tuple-element.91.rims, f32[2,17,32,512]{3,2,1,0:T(8,128)S(1)} %get-tuple-element.86.coefs, ...), custom_call_target="tpu_custom_call", output_to_operand_aliasing={{2}: (4, {}), {1}: (5, {}), {0}: (6, {})} | custom-call | flops 1 | bytes 1024 | tf_op jit(solution)/shard_map/last_rim/pallas_call | solution.py:548
Async XLA Ops:
  0.6 1.6 %copy-start = (f32[1,64,16,512]{3,2,1,0:T(8,128)S(1)}, f32[1,64,16,512]{3,2,1,0:T(8,128)}, u32[]{:S(2)}) copy-start(f32[1,64,16,512]{3,2,1,0:T(8,128)} %param.10) | copy-start | bytes 6291460
  2.3 10.2 %collective-permute-start = (f32[64,512]{1,0:T(8,128)S(1)}, f32[64,512]{1,0:T(8,128)S(1)}, u32[]{:S(2)}, u32[]{:S(2)}) collective-permute-start(f32[64,512]{1,0:T(8,128)S(1)} %get-tuple-element.56), channel_id=1, source_target_pairs={{0,1},{1,2},{2,3},{3,4},{4,5},{5,6},{6,7},{7,8},{8,9},{9,10},{10,1... | collective-permute-start | bytes 393224 | tf_op jit(solution)/shard_map/ppermute | solution.py:637
  4.4 1.6 %copy-start.2 = (f32[1,63,16,512]{3,2,1,0:T(8,128)S(1)}, f32[1,63,16,512]{3,2,1,0:T(8,128)}, u32[]{:S(2)}) copy-start(f32[1,63,16,512]{3,2,1,0:T(8,128)} %param.8) | copy-start | bytes 6193156
  9.9 5.2 %collective-permute-start.3 = (f32[48,512]{1,0:T(8,128)S(1)}, f32[48,512]{1,0:T(8,128)S(1)}, u32[]{:S(2)}, u32[]{:S(2)}) collective-permute-start(f32[48,512]{1,0:T(8,128)S(1)} %get-tuple-element.63), channel_id=1, source_target_pairs={{0,17},{1,16},{2,19},{3,18},{4,21},{5,20},{6,23},{7,22},{8,25},{9,... | collective-permute-start | bytes 294920 | tf_op jit(solution)/shard_map/ppermute | solution.py:637
  11.0 5.9 %collective-permute-start.4 = (f32[48,512]{1,0:T(8,128)S(1)}, f32[48,512]{1,0:T(8,128)S(1)}, u32[]{:S(2)}, u32[]{:S(2)}) collective-permute-start(f32[48,512]{1,0:T(8,128)S(1)} %get-tuple-element.64), channel_id=1, source_target_pairs={{0,31},{1,18},{2,17},{3,20},{4,19},{5,22},{6,21},{7,24},{8,23},{9,... | collective-permute-start | bytes 294920 | tf_op jit(solution)/shard_map/ppermute | solution.py:637
  12.0 3.0 %collective-permute-start.1 = (f32[5,8,512]{2,1,0:T(8,128)S(1)}, f32[5,8,512]{2,1,0:T(8,128)S(1)}, u32[]{:S(2)}, u32[]{:S(2)}) collective-permute-start(f32[5,8,512]{2,1,0:T(8,128)S(1)} %get-tuple-element.61), channel_id=1, source_target_pairs={{0,16},{1,17},{2,18},{3,19},{4,20},{5,21},{6,22},{7,23},{8,24},{9,... | collective-permute-start | bytes 245768 | tf_op jit(solution)/shard_map/ppermute | solution.py:637
  12.1 2.9 %collective-permute-start.2 = (f32[5,8,512]{2,1,0:T(8,128)S(1)}, f32[5,8,512]{2,1,0:T(8,128)S(1)}, u32[]{:S(2)}, u32[]{:S(2)}) collective-permute-start(f32[5,8,512]{2,1,0:T(8,128)S(1)} %get-tuple-element.62), channel_id=1, source_target_pairs={{0,16},{1,17},{2,18},{3,19},{4,20},{5,21},{6,22},{7,23},{8,24},{9,... | collective-permute-start | bytes 245768 | tf_op jit(solution)/shard_map/ppermute | solution.py:637
  12.6 4.3 %copy-start.3 = (s32[1,2,16,512]{3,2,1,0:T(8,128)S(1)}, s32[1,2,16,512]{3,2,1,0:T(8,128)}, u32[]{:S(2)}) copy-start(s32[1,2,16,512]{3,2,1,0:T(8,128)} %param.11) | copy-start | bytes 196612
  12.6 4.3 %copy-start.4 = (s32[1,2,16,512]{3,2,1,0:T(8,128)S(1)}, s32[1,2,16,512]{3,2,1,0:T(8,128)}, u32[]{:S(2)}) copy-start(s32[1,2,16,512]{3,2,1,0:T(8,128)} %param.12) | copy-start | bytes 196612
  15.0 8.3 %copy-start.1 = (f32[1,64,16,512]{3,2,1,0:T(8,128)S(1)}, f32[1,64,16,512]{3,2,1,0:T(8,128)}, u32[]{:S(2)}) copy-start(f32[1,64,16,512]{3,2,1,0:T(8,128)} %param.10) | copy-start | bytes 6291460
  18.2 35.8 %collective-permute-start.7 = (f32[4,2,32,512]{3,2,1,0:T(8,128)S(1)}, f32[4,2,32,512]{3,2,1,0:T(8,128)S(1)}, u32[]{:S(2)}, u32[]{:S(2)}) collective-permute-start(f32[4,2,32,512]{3,2,1,0:T(8,128)S(1)} %get-tuple-element.77), channel_id=1, source_target_pairs={{0,1},{1,0},{2,3},{3,2},{4,5},{5,4},{6,7},{7,6},{8,9},{9,8},{10,11... | collective-permute-start | bytes 1572872 | tf_op jit(solution)/shard_map/ppermute | solution.py:637
  19.5 34.6 %collective-permute-start.8 = (f32[4,2,32,512]{3,2,1,0:T(8,128)S(1)}, f32[4,2,32,512]{3,2,1,0:T(8,128)S(1)}, u32[]{:S(2)}, u32[]{:S(2)}) collective-permute-start(f32[4,2,32,512]{3,2,1,0:T(8,128)S(1)} %get-tuple-element.78), channel_id=1, source_target_pairs={{0,15},{1,2},{2,1},{3,4},{4,3},{5,6},{6,5},{7,8},{8,7},{9,10},{10,... | collective-permute-start | bytes 1572872 | tf_op jit(solution)/shard_map/ppermute | solution.py:637
  22.4 42.8 %collective-permute-start.5 = (f32[4,2,32,512]{3,2,1,0:T(8,128)S(1)}, f32[4,2,32,512]{3,2,1,0:T(8,128)S(1)}, u32[]{:S(2)}, u32[]{:S(2)}) collective-permute-start(f32[4,2,32,512]{3,2,1,0:T(8,128)S(1)} %get-tuple-element.74), channel_id=1, source_target_pairs={{0,1},{1,0},{2,3},{3,2},{4,5},{5,4},{6,7},{7,6},{8,9},{9,8},{10,11... | collective-permute-start | bytes 1572872 | tf_op jit(solution)/shard_map/ppermute | solution.py:637
  22.4 46.2 %collective-permute-start.6 = (f32[4,2,32,512]{3,2,1,0:T(8,128)S(1)}, f32[4,2,32,512]{3,2,1,0:T(8,128)S(1)}, u32[]{:S(2)}, u32[]{:S(2)}) collective-permute-start(f32[4,2,32,512]{3,2,1,0:T(8,128)S(1)} %get-tuple-element.75), channel_id=1, source_target_pairs={{0,15},{1,2},{2,1},{3,4},{4,3},{5,6},{6,5},{7,8},{8,7},{9,10},{10,... | collective-permute-start | bytes 1572872 | tf_op jit(solution)/shard_map/ppermute | solution.py:637
  56.7 41.4 %collective-permute-start.11 = (f32[4,2,32,512]{3,2,1,0:T(8,128)S(1)}, f32[4,2,32,512]{3,2,1,0:T(8,128)S(1)}, u32[]{:S(2)}, u32[]{:S(2)}) collective-permute-start(f32[4,2,32,512]{3,2,1,0:T(8,128)S(1)} %get-tuple-element.95), channel_id=1, source_target_pairs={{0,1},{1,0},{2,3},{3,2},{4,5},{5,4},{6,7},{7,6},{8,9},{9,8},{10,11... | collective-permute-start | bytes 1572872 | tf_op jit(solution)/shard_map/ppermute | solution.py:637
  56.8 41.3 %collective-permute-start.12 = (f32[4,2,32,512]{3,2,1,0:T(8,128)S(1)}, f32[4,2,32,512]{3,2,1,0:T(8,128)S(1)}, u32[]{:S(2)}, u32[]{:S(2)}) collective-permute-start(f32[4,2,32,512]{3,2,1,0:T(8,128)S(1)} %get-tuple-element.96), channel_id=1, source_target_pairs={{0,15},{1,2},{2,1},{3,4},{4,3},{5,6},{6,5},{7,8},{8,7},{9,10},{10,... | collective-permute-start | bytes 1572872 | tf_op jit(solution)/shard_map/ppermute | solution.py:637
  71.3 38.9 %collective-permute-start.9 = (f32[4,2,32,512]{3,2,1,0:T(8,128)S(1)}, f32[4,2,32,512]{3,2,1,0:T(8,128)S(1)}, u32[]{:S(2)}, u32[]{:S(2)}) collective-permute-start(f32[4,2,32,512]{3,2,1,0:T(8,128)S(1)} %get-tuple-element.92), channel_id=1, source_target_pairs={{0,1},{1,0},{2,3},{3,2},{4,5},{5,4},{6,7},{7,6},{8,9},{9,8},{10,11... | collective-permute-start | bytes 1572872 | tf_op jit(solution)/shard_map/ppermute | solution.py:637
  71.4 42.2 %collective-permute-start.10 = (f32[4,2,32,512]{3,2,1,0:T(8,128)S(1)}, f32[4,2,32,512]{3,2,1,0:T(8,128)S(1)}, u32[]{:S(2)}, u32[]{:S(2)}) collective-permute-start(f32[4,2,32,512]{3,2,1,0:T(8,128)S(1)} %get-tuple-element.93), channel_id=1, source_target_pairs={{0,15},{1,2},{2,1},{3,4},{4,3},{5,6},{6,5},{7,8},{8,7},{9,10},{10,... | collective-permute-start | bytes 1572872 | tf_op jit(solution)/shard_map/ppermute | solution.py:637
